TPU v7x, 32 devices: a whole 2x2x4 slice. The times are simulated.
32 devices in a mesh: groups: 2 (over y), dom: 4 (over z), case: 2 (over x), sub: 2 (over core).
Axes of the slice: x: 2, y: 2, z: 4, core: 2. Of those that a mesh axis runs over, the one named last changes fastest.
Arguments:
- node_feats: bfloat16 [4, 5120, 128], P(('groups', 'case'), 'dom'), parts along dimension 0, may hold values from -6 to 6
- cotangent: bfloat16 [4, 5120, 128], P(('groups', 'case'), 'dom'), parts along dimension 0, may hold values from -6 to 6
- block_counts: int32 [8], P(('groups', 'dom')), parts along dimension 0, may hold values from 2 to 10, as said below
- neighbours: int32 [80, 8], P(('groups', 'dom')), parts along dimension 0, may hold values from -1 to 17, as said below
- send_sets: int32 [32, 2], P(('groups', 'dom')), parts along dimension 0, may hold values from 0 to 9, as said below
- edge_w1: bfloat16 [256, 512], P(None, 'sub'), may hold values from -0.375 to 0.375
- edge_b1: float32 [512], P('sub'), may hold values from -3 to 3
- edge_w2: bfloat16 [512, 128], P('sub'), may hold values from -0.25 to 0.25
- node_w1: bfloat16 [256, 512], P(None, 'sub'), may hold values from -0.375 to 0.375
- node_b1: float32 [512], P('sub'), may hold values from -3 to 3
- node_w2: bfloat16 [512, 128], P('sub'), may hold values from -0.25 to 0.25
- norm_gain: float32 [128], replicated, may hold values from 0.5 to 2
Outputs:
- new_nodes: bfloat16 [4, 5120, 128], P(('groups', 'case'), 'dom'), parts along dimension 0
- node_grads: bfloat16 [4, 5120, 128], P(('groups', 'case'), 'dom'), parts along dimension 0
- d_edge_w1: float32 [512, 512], P('groups', 'sub'), parts along dimension 0
- d_edge_b1: float32 [1024], P(('groups', 'sub')), parts along dimension 0
- d_edge_w2: float32 [1024, 128], P(('groups', 'sub')), parts along dimension 0
- d_node_w1: float32 [512, 512], P('groups', 'sub'), parts along dimension 0
- d_node_b1: float32 [1024], P(('groups', 'sub')), parts along dimension 0
- d_node_w2: float32 [1024, 128], P(('groups', 'sub')), parts along dimension 0
- d_norm_gain: float32 [256], P('groups'), parts along dimension 0
There are 2 independent parts, one for each index of `groups`. A program takes and returns all parts, laid end to end along the dimension named above; an argument that names none is the same for every part. Nothing has to cross between parts.
Inputs may be any that keep to these rules, and one draw needn't show every extreme that they name: Blocks from block_counts[p] on are empty slots of partition p; some partition has 10 live blocks and some has 2. `neighbours`: Every entry of an empty block is -1 and no entry of a live block is. `send_sets`: row 4 p + j lists live blocks of partition p, repeats allowed, that partition p + d_j with d = (1, -1, 2, -2) receives.
All inputs are finite; a program needn't handle non-finite values.
Results may differ from a plain program's by a relative error of at most 0.009.
Values may be sent and summed in bfloat16 or wider, within the bound.
A program may use at most 64 MiB of HBM per device.

v0:
```python
import jax
import jax.numpy as jnp
from jax import lax
from jax.sharding import PartitionSpec as P

BLOCK = 128


DISTANCES = (1, -1, 2, -2)
EPSILON = 1e-05


def passed_along(block, axis, distance):
    devices = range(lax.axis_size(axis))
    route = [(i - distance, i) for i in devices if i - distance in devices]
    return lax.ppermute(block, axis, route)


def silu_slope(values):
    sigmoid = jax.nn.sigmoid(values)
    return sigmoid * (1.0 + values * (1.0 - sigmoid))


def normalize(values, norm_gain):
    centre = jnp.mean(values, axis=-1, keepdims=True)
    shifted = values - centre
    spread = jnp.mean(shifted * shifted, axis=-1, keepdims=True)
    return shifted * lax.rsqrt(spread + EPSILON) * norm_gain


def mask_edges(link_ids, alive_rows):
    present = (link_ids >= 0) & (alive_rows[:, None] > 0)
    return present.astype(jnp.float32)[:, :, None, None]


def on_device(
    node_feats,
    cotangent,
    block_counts,
    neighbours,
    send_sets,
    edge_w1,
    edge_b1,
    edge_w2,
    node_w1,
    node_b1,
    node_w2,
    norm_gain,
):
    feat_width = node_feats.shape[2]
    block_count, fan_out = neighbours.shape
    bound_count = send_sets.shape[1]
    extended_count = block_count + 4 * bound_count
    flat_nodes = node_feats[0]
    flat_cotangent = cotangent[0]
    features = flat_nodes.reshape(block_count, BLOCK, feat_width)
    alive_blocks = (jnp.arange(block_count) < block_counts[0]).astype(jnp.float32)
    outgoing = [features[send_sets[direction]] for direction in range(4)]
    ghosts = [
        passed_along(outgoing[direction], "dom", DISTANCES[direction]) for direction in range(4)
    ]
    extended = jnp.concatenate([features] + ghosts, axis=0)
    edge_first, edge_second, node_first, node_second = (edge_w1, edge_w2, node_w1, node_w2)
    edge_bias, node_bias = (edge_b1, node_b1)
    own_start = 0
    hidden_width = edge_first.shape[1]
    target_w1 = edge_first[:feat_width]
    source_w1 = edge_first[feat_width:]
    own_nodes = features.reshape(-1, feat_width)
    alive_nodes = jnp.repeat(alive_blocks, BLOCK)[:, None]
    group_size = 2
    group_count = block_count // group_size

    def edge_preact(targets, link_ids):
        sources = extended[jnp.maximum(link_ids, 0).reshape(-1)]
        pre_target = jnp.dot(
            targets.reshape(-1, feat_width), target_w1, preferred_element_type=jnp.float32
        )
        pre_source = jnp.dot(
            sources.reshape(-1, feat_width), source_w1, preferred_element_type=jnp.float32
        )
        pre_target = pre_target.reshape(group_size, 1, BLOCK, hidden_width)
        pre_source = pre_source.reshape(group_size, fan_out, BLOCK, hidden_width)
        return (pre_source + pre_target + edge_bias, sources)

    feature_groups = features.reshape(group_count, group_size, BLOCK, feat_width)
    link_groups = neighbours.reshape(group_count, group_size, fan_out)
    alive_groups = alive_blocks.reshape(group_count, group_size)

    def forward_step(totals, inputs_now):
        targets, link_ids, alive_rows = inputs_now
        preact, sources = edge_preact(targets, link_ids)
        activation = jax.nn.silu(preact) * mask_edges(link_ids, alive_rows)
        return (totals, jnp.sum(activation, axis=1).astype(jnp.bfloat16))

    _, summed = lax.scan(
        forward_step, jnp.zeros((), jnp.float32), (feature_groups, link_groups, alive_groups)
    )
    edge_sum = summed.reshape(-1, hidden_width)
    messages = lax.psum(
        jnp.dot(edge_sum, edge_second, preferred_element_type=jnp.float32), "sub"
    ).astype(jnp.bfloat16)
    node_preact = (
        jnp.dot(own_nodes, node_first[:feat_width], preferred_element_type=jnp.float32)
        + jnp.dot(messages, node_first[feat_width:], preferred_element_type=jnp.float32)
        + node_bias
    )
    node_hidden = jax.nn.silu(node_preact).astype(jnp.bfloat16)
    update = lax.psum(jnp.dot(node_hidden, node_second, preferred_element_type=jnp.float32), "sub")
    normed, norm_back = jax.vjp(normalize, update, norm_gain)
    own_new = (own_nodes.astype(jnp.float32) + alive_nodes * normed).astype(jnp.bfloat16)
    grad_normed = flat_cotangent.astype(jnp.float32) * alive_nodes
    grad_update, d_norm_gain = norm_back(grad_normed)
    grad_update = grad_update.astype(jnp.bfloat16)
    grad_hidden = jnp.dot(grad_update, node_second.T, preferred_element_type=jnp.float32)
    grad_node_pre = (grad_hidden * silu_slope(node_preact)).astype(jnp.bfloat16)
    d_node_w2 = jnp.dot(node_hidden.T, grad_update, preferred_element_type=jnp.float32)
    d_node_w1 = jnp.concatenate(
        [
            jnp.dot(own_nodes.T, grad_node_pre, preferred_element_type=jnp.float32),
            jnp.dot(messages.T, grad_node_pre, preferred_element_type=jnp.float32),
        ],
        axis=0,
    )
    d_node_b1 = jnp.sum(grad_node_pre.astype(jnp.float32), axis=0)
    grad_x_node = jnp.dot(
        grad_node_pre, node_first[:feat_width].T, preferred_element_type=jnp.float32
    )
    grad_messages = lax.psum(
        jnp.dot(grad_node_pre, node_first[feat_width:].T, preferred_element_type=jnp.float32), "sub"
    ).astype(jnp.bfloat16)
    d_node_w1, d_node_b1, d_node_w2, d_norm_gain = (d_node_w1, d_node_b1, d_node_w2, d_norm_gain)
    d_edge_w2 = jnp.dot(edge_sum.T, grad_messages, preferred_element_type=jnp.float32)
    grad_sum = jnp.dot(grad_messages, edge_second.T, preferred_element_type=jnp.float32)
    grad_groups = grad_sum.reshape(group_count, group_size, BLOCK, hidden_width)
    extended_ids = jnp.arange(extended_count)

    def backward_step(totals, inputs_now):
        targets, link_ids, alive_rows, upstream = inputs_now
        preact, sources = edge_preact(targets, link_ids)
        grad_pre = (
            upstream[:, None] * silu_slope(preact) * mask_edges(link_ids, alive_rows)
        ).astype(jnp.bfloat16)
        grad_rows = grad_pre.reshape(-1, hidden_width)
        target_total = totals[0] + jnp.einsum(
            "bif,bkih->fh", targets, grad_pre, preferred_element_type=jnp.float32
        )
        source_total = totals[1] + jnp.einsum(
            "ef,eh->fh",
            sources.reshape(-1, feat_width),
            grad_rows,
            preferred_element_type=jnp.float32,
        )
        bias_total = totals[2] + jnp.sum(grad_rows.astype(jnp.float32), axis=0)
        spread_grad = jnp.dot(grad_rows, source_w1.T, preferred_element_type=jnp.float32).reshape(
            group_size * fan_out, BLOCK * feat_width
        )
        one_hot = (link_ids.reshape(-1)[None, :] == extended_ids[:, None]).astype(jnp.float32)
        extended_total = totals[3] + jnp.dot(
            one_hot, spread_grad, precision=lax.Precision.HIGHEST
        ).reshape(extended_count, BLOCK, feat_width)
        target_part = jnp.sum(grad_pre.astype(jnp.float32), axis=1).astype(jnp.bfloat16)
        return ((target_total, source_total, bias_total, extended_total), target_part)

    start_totals = (
        jnp.zeros((feat_width, hidden_width), jnp.float32),
        jnp.zeros((feat_width, hidden_width), jnp.float32),
        jnp.zeros((hidden_width,), jnp.float32),
        jnp.zeros((extended_count, BLOCK, feat_width), jnp.float32),
    )
    edge_totals, target_parts = lax.scan(
        backward_step, start_totals, (feature_groups, link_groups, alive_groups, grad_groups)
    )
    d_edge_w1 = jnp.concatenate([edge_totals[0], edge_totals[1]], axis=0)
    d_edge_b1 = edge_totals[2]
    extended_grad = edge_totals[3]
    target_grad = target_parts.reshape(-1, hidden_width)
    grad_x_target = jnp.dot(target_grad, target_w1.T, preferred_element_type=jnp.float32)
    ghost_grad = [
        extended_grad[
            block_count + direction * bound_count : block_count + (direction + 1) * bound_count
        ]
        for direction in range(4)
    ]
    returned = [
        passed_along(
            ghost_grad[direction].astype(jnp.bfloat16), "dom", -DISTANCES[direction]
        ).astype(jnp.float32)
        for direction in range(4)
    ]
    returned_rows = jnp.concatenate(returned, axis=0).reshape(4 * bound_count, BLOCK * feat_width)
    owner_hot = (jnp.arange(block_count)[:, None] == send_sets.reshape(-1)[None, :]).astype(
        jnp.float32
    )
    owned_grad = jnp.dot(owner_hot, returned_rows, precision=lax.Precision.HIGHEST).reshape(
        -1, feat_width
    )
    local_grad = extended_grad[:block_count].reshape(-1, feat_width)
    partial_grad = local_grad + owned_grad
    own_rows = partial_grad + grad_x_node + grad_x_target
    partial_grad = lax.dynamic_update_slice_in_dim(partial_grad, own_rows, own_start * BLOCK, 0)
    node_grads = (lax.psum(partial_grad, "sub") + flat_cotangent.astype(jnp.float32)).astype(
        jnp.bfloat16
    )
    d_edge_w1, d_edge_b1, d_edge_w2 = (d_edge_w1, d_edge_b1, d_edge_w2)
    summed_grads = lax.psum(
        (d_edge_w1, d_edge_b1, d_edge_w2, d_node_w1, d_node_b1, d_node_w2, d_norm_gain),
        ("dom", "case"),
    )
    return (
        own_new[None],
        node_grads[None],
        summed_grads[0],
        summed_grads[1],
        summed_grads[2],
        summed_grads[3],
        summed_grads[4],
        summed_grads[5],
        summed_grads[6],
    )


def solution(mesh):
    placed = (
        P(("groups", "case"), "dom", None),
        P(("groups", "case"), "dom", None),
        P(("groups", "dom")),
        P(("groups", "dom"), None),
        P(("groups", "dom"), None),
        P(None, "sub"),
        P("sub"),
        P("sub", None),
        P(None, "sub"),
        P("sub"),
        P("sub", None),
        P(),
    )
    return jax.shard_map(
        on_device,
        mesh=mesh,
        in_specs=placed,
        out_specs=(
            P(("groups", "case"), "dom", None),
            P(("groups", "case"), "dom", None),
            P("groups", "sub"),
            P(("groups", "sub")),
            P(("groups", "sub"), None),
            P("groups", "sub"),
            P(("groups", "sub")),
            P(("groups", "sub"), None),
            P("groups"),
        ),
        check_vma=False,
    )
```

profile of v0, /device:TPU:0, one launch (start us, length us, event | category | flops | bytes accessed | tf_op | source)
XLA Modules:
  0.0 293.6 jit_solution(16444586638354938280)
XLA Ops:
  9.9 4.9 %collective-permute-start = (bf16[2,128,128]{2,1,0:T(8,128)(2,1)S(1)}, bf16[2,128,128]{2,1,0:T(8,128)(2,1)S(1)}, u32[]{:S(2)}, u32[]{:S(2)}) collective-permute-start(bf16[2,128,128]{2,1,0:T(8,128)(2,1)S(1)} %gather_fusion.2), channel_id=1, source_target_pairs={{0,4},{4,8},{8,12},{1,5},{5,9},{9,13},{2,6},{6,10},{10,14},{3,7},{... | collective-permute-start | bytes 196616 | tf_op jit(solution)/shard_map/ppermute | solution.py:16
  16.4 4.5 %collective-permute-start.2 = (bf16[2,128,128]{2,1,0:T(8,128)(2,1)S(1)}, bf16[2,128,128]{2,1,0:T(8,128)(2,1)S(1)}, u32[]{:S(2)}, u32[]{:S(2)}) collective-permute-start(bf16[2,128,128]{2,1,0:T(8,128)(2,1)S(1)} %gather_fusion.4), channel_id=1, source_target_pairs={{0,8},{4,12},{1,9},{5,13},{2,10},{6,14},{3,11},{7,15},{16,24},{20,... | collective-permute-start | bytes 196616 | tf_op jit(solution)/shard_map/ppermute | solution.py:16
  29.9 2.2 fusion.38
  33.1 16.4 %while.29 = (s32[]{:T(128)}, bf16[5,2,128,256]{3,2,1,0:T(8,128)(2,1)S(1)}, s32[5,2,8]{2,1,0:T(2,128)S(1)}, bf16[18,128,128]{2,1,0:T(8,128)(2,1)S(1)}, bf16[128,2...) while((s32[]{:T(128)}, ...), condition=%wide.region_2.3_spmd, body=%wide.region_0.2_spmd.sunk | while | flops 155124800 | bytes 2692813 | solution.py:96
  49.9 5.2 %all-reduce.13 = bf16[1280,128]{1,0:T(8,128)(2,1)S(1)} all-reduce(f32[1280,128]{1,0:T(8,128)S(1)} %fusion.73), channel_id=1, replica_groups=mesh['groups'=2,'dom'=4,'case'=2,'sub'=2] {'sub'}, use_global_device_ids=true, to_apply=%region_3.4 | all-reduce | flops 163840 | bytes 983040 | tf_op jit(solution)/shard_map/psum | solution.py:100
  55.1 2.8 multiply_convert_fusion.1
  60.8 21.3 %all-reduce.8.cloned.1.call-done = f32[1280,128]{1,0:T(8,128)} async-done(((f32[1280,128]{1,0:T(8,128)}), f32[1280,128]{1,0:T(8,128)}) %all-reduce.8.cloned.1.call-update) | async-done | bytes 655376 | tf_op jit(solution)/shard_map/psum | solution.py:109
  90.6 5.2 %all-reduce.14 = bf16[1280,128]{1,0:T(8,128)(2,1)S(1)} all-reduce(f32[1280,128]{1,0:T(8,128)S(1)} %fusion.54), channel_id=1, replica_groups=mesh['groups'=2,'dom'=4,'case'=2,'sub'=2] {'sub'}, use_global_device_ids=true, to_apply=%region_9.10 | all-reduce | flops 163840 | bytes 983040 | tf_op jit(solution)/shard_map/psum | solution.py:129
  97.1 62.2 %while.30 = (s32[]{:T(128)}, f32[128,256]{1,0:T(8,128)}, f32[128,256]{1,0:T(8,128)}, f32[256]{0:T(256)S(1)}, f32[18,128,128]{2,0,1:T(8,128)}, /*index=5*/bf16[5,...) while((s32[]{:T(128)}, f32[128,256]{1,0:T(8,128)}, ...), condition=%wide.region_13.14_spmd.clone, body=%wide.region_10.13_spmd.clone.sunk | while | flops 501352032 | bytes 26290612 | solution.py:171
  100.0 2.2 convert_reduce_fusion.4
  104.8 2.1 select_add_fusion.5
  110.6 2.2 convert_reduce_fusion.4
  116.3 3.6 %select_add_fusion.5 = f32[18,128,128]{2,0,1:T(8,128)} fusion(f32[18,128,128]{2,0,1:T(8,128)} %get-tuple-element.471, pred[]{:T(512)S(6)} %compare.3, s32[16]{0:T(128)S(1)} %copy-done.32, f32[16,16384]{1,0:T(8,128)S(1)} %reshape.434), kind=kOutput, calls=%fused_computation.25.clone.1 | convolution fusion | flops 57213216 | bytes 3407937 | tf_op jit(solution)/shard_map/while/body/eval_jaxpr/dot_general | solution.py:159
  123.5 2.2 convert_reduce_fusion.4
  129.2 3.6 %select_add_fusion.5 = f32[18,128,128]{2,0,1:T(8,128)} fusion(f32[18,128,128]{2,0,1:T(8,128)} %get-tuple-element.471, pred[]{:T(512)S(6)} %compare.3, s32[16]{0:T(128)S(1)} %copy-done.32, f32[16,16384]{1,0:T(8,128)S(1)} %reshape.434), kind=kOutput, calls=%fused_computation.25.clone.1 | convolution fusion | flops 57213216 | bytes 3407937 | tf_op jit(solution)/shard_map/while/body/eval_jaxpr/dot_general | solution.py:159
  136.4 2.2 convert_reduce_fusion.4
  142.1 3.6 %select_add_fusion.5 = f32[18,128,128]{2,0,1:T(8,128)} fusion(f32[18,128,128]{2,0,1:T(8,128)} %get-tuple-element.471, pred[]{:T(512)S(6)} %compare.3, s32[16]{0:T(128)S(1)} %copy-done.32, f32[16,16384]{1,0:T(8,128)S(1)} %reshape.434), kind=kOutput, calls=%fused_computation.25.clone.1 | convolution fusion | flops 57213216 | bytes 3407937 | tf_op jit(solution)/shard_map/while/body/eval_jaxpr/dot_general | solution.py:159
  149.4 2.2 convert_reduce_fusion.4
  155.1 3.6 %select_add_fusion.5 = f32[18,128,128]{2,0,1:T(8,128)} fusion(f32[18,128,128]{2,0,1:T(8,128)} %get-tuple-element.471, pred[]{:T(512)S(6)} %compare.3, s32[16]{0:T(128)S(1)} %copy-done.32, f32[16,16384]{1,0:T(8,128)S(1)} %reshape.434), kind=kOutput, calls=%fused_computation.25.clone.1 | convolution fusion | flops 57213216 | bytes 3407937 | tf_op jit(solution)/shard_map/while/body/eval_jaxpr/dot_general | solution.py:159
  162.5 5.8 %collective-permute-start.7 = (bf16[2,128,128]{2,0,1:T(2,128)(2,1)S(1)}, bf16[2,128,128]{2,0,1:T(2,128)(2,1)S(1)}, u32[]{:S(2)}, u32[]{:S(2)}) collective-permute-start(bf16[2,128,128]{2,0,1:T(2,128)(2,1)S(1)} %get-tuple-element.257), channel_id=1, source_target_pairs={{0,8},{4,12},{1,9},{5,13},{2,10},{6,14},{3,11},{7,15},{16,24},{20,... | collective-permute-start | bytes 196616 | tf_op jit(solution)/shard_map/ppermute | solution.py:16
  169.7 3.6 %collective-permute-start.5 = (bf16[2,128,128]{2,0,1:T(2,128)(2,1)S(1)}, bf16[2,128,128]{2,0,1:T(2,128)(2,1)S(1)}, u32[]{:S(2)}, u32[]{:S(2)}) collective-permute-start(bf16[2,128,128]{2,0,1:T(2,128)(2,1)S(1)} %get-tuple-element.259), channel_id=1, source_target_pairs={{0,4},{4,8},{8,12},{1,5},{5,9},{9,13},{2,6},{6,10},{10,14},{3,7},{... | collective-permute-start | bytes 196616 | tf_op jit(solution)/shard_map/ppermute | solution.py:16
  183.4 23.1 %all-reduce = (f32[256]{0:T(256)}, f32[256]{0:T(256)}, f32[128]{0:T(128)}) all-reduce(f32[256]{0:T(256)S(1)} %get-tuple-element.142, f32[256]{0:T(256)S(1)} %copy-done.36, f32[128]{0:T(128)S(1)} %copy-done.34), channel_id=1, replica_groups=mesh['groups'=2,'dom'=4,'case'=2,'sub'=2] {'dom','case'}, use_global_device_ids=true, to_apply=%region_16.17 | all-reduce | flops 640 | bytes 5120 | tf_op jit(solution)/shard_map/psum | solution.py:206
  206.6 1.9 fusion.36
  208.4 72.1 %all-reduce.12.cloned.1.call-done = (f32[256,256]{1,0:T(8,128)}, f32[256,128]{1,0:T(8,128)}, f32[256,256]{1,0:T(8,128)}, f32[256,128]{1,0:T(8,128)}) async-done(((f32[256,256]{1,0:T(8,128)}, f32[256,128]{1,0:T(8,128)}, f32[256,256]{1,0:T(8,128)}, f32[256,128]{1,0:T(8,128)}), (f32[256,256]{1,0:T(8,128)}, f32[256,128]{1,0:T(8,128)}, f32[256,256]{1,0:T(8,128)}, ...) | async-done | bytes 786448 | tf_op jit(solution)/shard_map/psum | solution.py:206
  (327 shorter events, 97.6 us)
Async XLA Ops:
  7.2 51.6 %copy-start = (bf16[256,128]{1,0:T(8,128)(2,1)S(1)}, bf16[256,128]{1,0:T(8,128)(2,1)}, u32[]{:S(2)}) copy-start(bf16[256,128]{1,0:T(8,128)(2,1)} %param.26) | copy-start | bytes 196612
  7.2 22.7 %copy-start.2 = (bf16[1,1280,128]{2,1,0:T(8,128)(2,1)S(1)}, bf16[1,1280,128]{2,1,0:T(8,128)(2,1)}, u32[]{:S(2)}) copy-start(bf16[1,1280,128]{2,1,0:T(8,128)(2,1)} %param.16) | copy-start | bytes 983044
  7.2 75.0 %all-reduce.8.cloned.1.call-start = ((), (), s32[]{:S(2)}) async-start(), calls=%async_computation | async-start | bytes 1310720 | tf_op jit(solution)/shard_map/psum | solution.py:109
  9.9 22.9 %collective-permute-start = (bf16[2,128,128]{2,1,0:T(8,128)(2,1)S(1)}, bf16[2,128,128]{2,1,0:T(8,128)(2,1)S(1)}, u32[]{:S(2)}, u32[]{:S(2)}) collective-permute-start(bf16[2,128,128]{2,1,0:T(8,128)(2,1)S(1)} %gather_fusion.2), channel_id=1, source_target_pairs={{0,4},{4,8},{8,12},{1,5},{5,9},{9,13},{2,6},{6,10},{10,14},{3,7},{... | collective-permute-start | bytes 196616 | tf_op jit(solution)/shard_map/ppermute | solution.py:16
  16.4 16.4 %collective-permute-start.2 = (bf16[2,128,128]{2,1,0:T(8,128)(2,1)S(1)}, bf16[2,128,128]{2,1,0:T(8,128)(2,1)S(1)}, u32[]{:S(2)}, u32[]{:S(2)}) collective-permute-start(bf16[2,128,128]{2,1,0:T(8,128)(2,1)S(1)} %gather_fusion.4), channel_id=1, source_target_pairs={{0,8},{4,12},{1,9},{5,13},{2,10},{6,14},{3,11},{7,15},{16,24},{20,... | collective-permute-start | bytes 196616 | tf_op jit(solution)/shard_map/ppermute | solution.py:16
  22.4 10.3 %collective-permute-start.1 = (bf16[2,128,128]{2,1,0:T(8,128)(2,1)S(1)}, bf16[2,128,128]{2,1,0:T(8,128)(2,1)S(1)}, u32[]{:S(2)}, u32[]{:S(2)}) collective-permute-start(bf16[2,128,128]{2,1,0:T(8,128)(2,1)S(1)} %gather_fusion.3), channel_id=1, source_target_pairs={{4,0},{8,4},{12,8},{5,1},{9,5},{13,9},{6,2},{10,6},{14,10},{7,3},{... | collective-permute-start | bytes 196616 | tf_op jit(solution)/shard_map/ppermute | solution.py:16
  25.3 7.8 %collective-permute-start.3 = (bf16[2,128,128]{2,1,0:T(8,128)(2,1)S(1)}, bf16[2,128,128]{2,1,0:T(8,128)(2,1)S(1)}, u32[]{:S(2)}, u32[]{:S(2)}) collective-permute-start(bf16[2,128,128]{2,1,0:T(8,128)(2,1)S(1)} %gather_fusion.5), channel_id=1, source_target_pairs={{8,0},{12,4},{9,1},{13,5},{10,2},{14,6},{11,3},{15,7},{24,16},{28,... | collective-permute-start | bytes 196616 | tf_op jit(solution)/shard_map/ppermute | solution.py:16
  33.1 16.4 %copy-start.28 = (bf16[256,128]{1,0:T(8,128)(2,1)S(1)}, bf16[256,128]{1,0:T(8,128)(2,1)}, u32[]{:S(2)}) copy-start(bf16[256,128]{1,0:T(8,128)(2,1)} %param.23) | copy-start | bytes 196612
  49.5 8.4 %copy-start.6 = (bf16[5,2,128,256]{3,2,1,0:T(8,128)(2,1)}, bf16[5,2,128,256]{3,2,1,0:T(8,128)(2,1)S(1)}, u32[]{:S(2)}) copy-start(bf16[5,2,128,256]{3,2,1,0:T(8,128)(2,1)S(1)} %get-tuple-element.137) | copy-start | bytes 1966084
  49.5 8.4 %copy-start.22 = (bf16[128,256]{1,0:T(8,128)(2,1)}, bf16[128,256]{1,0:T(8,128)(2,1)S(1)}, u32[]{:S(2)}) copy-start(bf16[128,256]{1,0:T(8,128)(2,1)S(1)} %get-tuple-element.527) | copy-start | bytes 196612
  49.5 5.5 %copy-start.26 = (bf16[256,256]{1,0:T(8,128)(2,1)S(1)}, bf16[256,256]{1,0:T(8,128)(2,1)}, u32[]{:S(2)}) copy-start(bf16[256,256]{1,0:T(8,128)(2,1)} %param.24) | copy-start | bytes 393220
  49.5 5.5 %copy-start.37 = (f32[256]{0:T(256)S(1)}, f32[256]{0:T(256)}, u32[]{:S(2)}) copy-start(f32[256]{0:T(256)} %param.25) | copy-start | bytes 3076
  58.7 26.4 %copy-start.13 = (bf16[1,1280,128]{2,1,0:T(8,128)(2,1)S(1)}, bf16[1,1280,128]{2,1,0:T(8,128)(2,1)}, u32[]{:S(2)}) copy-start(bf16[1,1280,128]{2,1,0:T(8,128)(2,1)} %param.17) | copy-start | bytes 983044
  58.7 26.4 %copy-start.33 = (f32[128]{0:T(128)S(1)}, f32[128]{0:T(128)}, u32[]{:S(2)}) copy-start(f32[128]{0:T(128)} %param.27) | copy-start | bytes 1540
  60.0 146.6 %all-reduce.10.cloned.1.call-start = ((), (), s32[]{:S(2)}) async-start(), calls=%async_computation.1 | async-start | bytes 1310720 | tf_op jit(solution)/shard_map/psum | solution.py:202
  107.6 5.1 %copy-start.8 = (f32[5,2,128,256]{3,2,1,0:T(8,128)}, f32[5,2,128,256]{3,2,1,0:T(8,128)S(1)}, u32[]{:S(2)}) copy-start(f32[5,2,128,256]{3,2,1,0:T(8,128)S(1)} %get-tuple-element.490) | copy-start | bytes 3932164 | tf_op jit(solution)/shard_map/while
  159.3 13.9 %copy-start.5 = (bf16[1280,256]{1,0:T(8,128)(2,1)S(1)}, bf16[1280,256]{1,0:T(8,128)(2,1)}, u32[]{:S(2)}) copy-start(bf16[1280,256]{1,0:T(8,128)(2,1)} %copy-done.4) | copy-start | bytes 1966084
  159.3 14.2 %copy-start.1 = (f32[18,128,128]{2,0,1:T(8,128)S(1)}, f32[18,128,128]{2,0,1:T(8,128)}, u32[]{:S(2)}) copy-start(f32[18,128,128]{2,0,1:T(8,128)} %get-tuple-element.138) | copy-start | bytes 3538948
  161.2 12.7 %collective-permute-start.4 = (bf16[2,128,128]{2,0,1:T(2,128)(2,1)S(1)}, bf16[2,128,128]{2,0,1:T(2,128)(2,1)S(1)}, u32[]{:S(2)}, u32[]{:S(2)}) collective-permute-start(bf16[2,128,128]{2,0,1:T(2,128)(2,1)S(1)} %get-tuple-element.256), channel_id=1, source_target_pairs={{4,0},{8,4},{12,8},{5,1},{9,5},{13,9},{6,2},{10,6},{14,10},{7,3},{... | collective-permute-start | bytes 196616 | tf_op jit(solution)/shard_map/ppermute | solution.py:16
  162.5 11.4 %collective-permute-start.7 = (bf16[2,128,128]{2,0,1:T(2,128)(2,1)S(1)}, bf16[2,128,128]{2,0,1:T(2,128)(2,1)S(1)}, u32[]{:S(2)}, u32[]{:S(2)}) collective-permute-start(bf16[2,128,128]{2,0,1:T(2,128)(2,1)S(1)} %get-tuple-element.257), channel_id=1, source_target_pairs={{0,8},{4,12},{1,9},{5,13},{2,10},{6,14},{3,11},{7,15},{16,24},{20,... | collective-permute-start | bytes 196616 | tf_op jit(solution)/shard_map/ppermute | solution.py:16
  168.3 7.4 %collective-permute-start.6 = (bf16[2,128,128]{2,0,1:T(2,128)(2,1)S(1)}, bf16[2,128,128]{2,0,1:T(2,128)(2,1)S(1)}, u32[]{:S(2)}, u32[]{:S(2)}) collective-permute-start(bf16[2,128,128]{2,0,1:T(2,128)(2,1)S(1)} %get-tuple-element.258), channel_id=1, source_target_pairs={{8,0},{12,4},{9,1},{13,5},{10,2},{14,6},{11,3},{15,7},{24,16},{28,... | collective-permute-start | bytes 196616 | tf_op jit(solution)/shard_map/ppermute | solution.py:16
  169.7 6.1 %collective-permute-start.5 = (bf16[2,128,128]{2,0,1:T(2,128)(2,1)S(1)}, bf16[2,128,128]{2,0,1:T(2,128)(2,1)S(1)}, u32[]{:S(2)}, u32[]{:S(2)}) collective-permute-start(bf16[2,128,128]{2,0,1:T(2,128)(2,1)S(1)} %get-tuple-element.259), channel_id=1, source_target_pairs={{0,4},{4,8},{8,12},{1,5},{5,9},{9,13},{2,6},{6,10},{10,14},{3,7},{... | collective-permute-start | bytes 196616 | tf_op jit(solution)/shard_map/ppermute | solution.py:16
  178.7 101.9 %all-reduce.12.cloned.1.call-start = ((), (), s32[]{:S(2)}) async-start(), calls=%async_computation.2 | async-start | bytes 1572864 | tf_op jit(solution)/shard_map/psum | solution.py:206
  181.1 25.5 %copy-start.14 = (bf16[1,1280,128]{2,1,0:T(8,128)(2,1)S(1)}, bf16[1,1280,128]{2,1,0:T(8,128)(2,1)}, u32[]{:S(2)}) copy-start(bf16[1,1280,128]{2,1,0:T(8,128)(2,1)} %param.17) | copy-start | bytes 983044
  (50 other events, 114.0 us)
Sparse Core Ops, SparseCore 0:
  60.1 22.0 all-reduce.7
  178.8 21.0 all-reduce.9
  204.2 76.3 all-reduce.11
where the time goes:
time: 295 us; the launch traced here: 294 us
  waiting for transfers between devices  95.6 us (32%)
  matrix products  62.6 us (21%)
  local copies, waits for them, and re-layouts  38.8 us (13%)
  blocking collectives  33.5 us (11%)
  starting transfers between devices  24.1 us (8%)
  other arithmetic  23.1 us (8%)
  between operations  15 us (5%)
    psum x1, waiting for transfers between devices, on_device(): lax.psum((d_edge_w1, d_edge_b1, d_edge_w2, d_node_w1, d_node_b1, d_node_w...  72.1 us
    ppermute x8, starting transfers between devices, passed_along(): return lax.ppermute(block, axis, route)  24 us
    psum x1, blocking collectives, on_device(): lax.psum((d_edge_w1, d_edge_b1, d_edge_w2, d_node_w1, d_node_b1, d_node_w...  23.1 us
    psum x1, waiting for transfers between devices, on_device(): lax.psum(jnp.dot(node_hidden, node_second, preferred_element_type=jnp.flo...  21.3 us
    dot_general x10, matrix products, edge_preact(): jnp.dot(sources.reshape(-1, feat_width), source_w1, preferred_element_typ...  18.5 us
    dot_general x5, matrix products, backward_step(): jnp.dot(one_hot, spread_grad, precision=lax.Precision.HIGHEST)  16.5 us
    unnamed x76, local copies, waits for them, and re-layouts  10 us
    dot_general x5, matrix products, backward_step(): jnp.einsum('bif,bkih->fh', targets, grad_pre, preferred_element_type=jnp....  7.96 us
  transfers between devices with their start and end apart: 11, of which 4 were waited for; matrix products, arithmetic and copies ran while one was open for 6% of the time, Pallas kernels for 0%

commit v1 on v0

v1 whole, which is shorter than its diff:
```python
import functools

import jax
import jax.numpy as jnp
from jax import lax
from jax.experimental import pallas as pl
from jax.experimental.pallas import tpu as pltpu
from jax.sharding import PartitionSpec as P

BLOCK = 128
CHUNK = 16
DISTANCES = (1, -1, 2, -2)
EPSILON = 1e-05
MESH = pl.DeviceIdType.MESH
BF = jnp.bfloat16
F32 = jnp.float32


def dot_nn(a, b):
    return lax.dot_general(a, b, (((1,), (0,)), ((), ())), preferred_element_type=F32)


def dot_nt(a, b):
    return lax.dot_general(a, b, (((1,), (1,)), ((), ())), preferred_element_type=F32)


def dot_tn(a, b):
    return lax.dot_general(a, b, (((0,), (0,)), ((), ())), preferred_element_type=F32)


def inside(position, count):
    return (position >= 0) & (position < count)


def remote(src, dst, send_sem, recv_sem, device):
    return pltpu.make_async_remote_copy(
        src_ref=src,
        dst_ref=dst,
        send_sem=send_sem,
        recv_sem=recv_sem,
        device_id=device,
        device_id_type=MESH,
    )


def gather_kernel(dom_count, bound, *refs):
    send, feats = refs[:2]
    mine = refs[2:8]
    ghosts = refs[8]
    others = refs[9:15]
    stage, half_send, half_recv, ghost_send, ghost_recv = refs[15:]
    here = lax.axis_index("dom")
    twin = {"sub": 1 - lax.axis_index("sub")}
    span = bound * BLOCK
    barrier = pltpu.get_barrier_semaphore()
    pl.semaphore_signal(barrier, inc=1, device_id=twin, device_id_type=MESH)
    expected = 1
    for distance in DISTANCES:
        there = here + distance
        present = inside(there, dom_count)
        expected = expected + jnp.where(present, 1, 0)

        @pl.when(present)
        def _():
            pl.semaphore_signal(barrier, inc=1, device_id={"dom": there}, device_id_type=MESH)

    for j in range(4):
        for m in range(bound):
            stage[j, m * BLOCK : (m + 1) * BLOCK, :] = feats[send[j, m]]
    pl.semaphore_wait(barrier, expected)

    def ghost_copy(j, there):
        return remote(
            stage.at[j],
            ghosts.at[pl.ds(j * span, span)],
            ghost_send.at[j],
            ghost_recv.at[j],
            {"dom": there},
        )

    for j in (2, 3, 0, 1):
        there = here + DISTANCES[j]

        @pl.when(inside(there, dom_count))
        def _():
            ghost_copy(j, there).start()

    halves = [
        remote(mine[n], others[n], half_send.at[n], half_recv.at[n], twin) for n in range(6)
    ]
    for copy in halves:
        copy.start()
    for j in range(4):

        @pl.when(jnp.logical_not(inside(here - DISTANCES[j], dom_count)))
        def _():
            ghosts[j * span : (j + 1) * span, :] = jnp.zeros((span, ghosts.shape[1]), BF)

    for copy in halves:
        copy.wait()
    for j in range(4):

        @pl.when(inside(here - DISTANCES[j], dom_count))
        def _():
            ghost_copy(j, here - DISTANCES[j]).wait_recv()

        @pl.when(inside(here + DISTANCES[j], dom_count))
        def _():
            ghost_copy(j, here + DISTANCES[j]).wait_send()


def layer_kernel(counts, links, feats, cot, ghosts, *refs):
    (ew1, oew1, eb1, oeb1, ew2, oew2, nw1, onw1, nb1, onb1, nw2, onw2, gain) = refs[:13]
    (new_o, part_o, ghost_o, mine_o, other_o) = refs[13:18]
    (
        w1h, w1f, w2f, n1f, n2f, psrc, ptgt, slope, gacc, gsum, esum, pair, hidden, gupd, gnode,
        gmsg, tgrad, gxnode, dsrc, dgain,
    ) = refs[18:]
    core = lax.axis_index("sub")
    block_count, fan = links.shape
    width = feats.shape[1]
    quarter = ew1.shape[1]
    own = block_count // 2
    ghost_count = ghosts.shape[0] // BLOCK

    def block_rows(b):
        return pl.ds(pl.multiple_of(b * BLOCK, BLOCK), BLOCK)

    w1f[:, :quarter] = ew1[...]
    w1f[:, quarter:] = oew1[...]
    w1h[...] = w1f[...] * jnp.asarray(0.5, BF)
    n1f[:, :quarter] = nw1[...]
    n1f[:, quarter:] = onw1[...]
    w2f[:quarter, :] = ew2[...]
    w2f[quarter:, :] = oew2[...]
    n2f[:quarter, :] = nw2[...]
    n2f[quarter:, :] = onw2[...]
    edge_bias = jnp.concatenate([eb1[...], oeb1[...]], axis=1) * 0.5
    node_bias = jnp.concatenate([nb1[...], onb1[...]], axis=1)
    gain_row = gain[...]
    dgain[...] = jnp.zeros_like(dgain)
    dsrc[...] = jnp.zeros_like(dsrc)

    @pl.loop(0, block_count)
    def _(b):
        psrc[b] = dot_nn(feats[block_rows(b), :], w1h[width:, :])
        gacc[b] = jnp.zeros(gacc.shape[1:], F32)

    @pl.loop(0, ghost_count)
    def _(b):
        psrc[block_count + b] = dot_nn(ghosts[block_rows(b), :], w1h[width:, :])
        gacc[block_count + b] = jnp.zeros(gacc.shape[1:], F32)

    @pl.loop(0, own)
    def _(i):
        b = core * own + i
        alive = jnp.where(b < counts[0], 1.0, 0.0)
        ids = [jnp.maximum(links[b, k], 0) for k in range(fan)]
        rows_i = block_rows(i)
        targets = feats[block_rows(b), :]
        ptgt[...] = dot_nn(targets, w1h[:width, :]) + edge_bias

        @pl.loop(0, BLOCK // CHUNK)
        def _(r):
            rows = pl.ds(pl.multiple_of(r * CHUNK, CHUNK), CHUNK)
            base = ptgt[rows, :]
            total = jnp.zeros_like(base)
            for k in range(fan):
                h = psrc[ids[k], rows, :] + base
                t = jnp.tanh(h)
                a = 1.0 + t
                q = h * a
                total = total + q
                slope[k, rows, :] = (a + q * (1.0 - t)).astype(BF)
            esum[pl.ds(pl.multiple_of(i * BLOCK + r * CHUNK, CHUNK), CHUNK), :] = (
                total * alive
            ).astype(BF)

        message = dot_nn(esum[rows_i, :], w2f[...]).astype(BF)
        pair[rows_i, :width] = targets
        pair[rows_i, width:] = message
        h = (dot_nn(pair[rows_i, :], n1f[...]) + node_bias) * 0.5
        t = jnp.tanh(h)
        a = 1.0 + t
        q = h * a
        node_slope = 0.5 * (a + q * (1.0 - t))
        hidden[rows_i, :] = q.astype(BF)
        update = dot_nn(hidden[rows_i, :], n2f[...])
        shifted = update - jnp.mean(update, axis=-1, keepdims=True)
        spread = jnp.mean(shifted * shifted, axis=-1, keepdims=True)
        scale = lax.rsqrt(spread + EPSILON)
        unit = shifted * scale
        new_o[rows_i, :] = (targets.astype(F32) + alive * (unit * gain_row)).astype(BF)
        seed = cot[block_rows(b), :].astype(F32) * alive
        dgain[...] += jnp.sum(seed * unit, axis=0, keepdims=True)
        seed = seed * gain_row
        grad = scale * (
            seed
            - jnp.mean(seed, axis=-1, keepdims=True)
            - unit * jnp.mean(seed * unit, axis=-1, keepdims=True)
        )
        gupd[rows_i, :] = grad.astype(BF)
        gnode[rows_i, :] = (dot_nt(gupd[rows_i, :], n2f[...]) * node_slope).astype(BF)
        back = dot_nt(gnode[rows_i, :], n1f[...])
        gxnode[rows_i, :] = back[:, :width] + cot[block_rows(b), :].astype(F32)
        gmsg[rows_i, :] = back[:, width:].astype(BF)
        gsum[...] = dot_nt(gmsg[rows_i, :], w2f[...]) * (0.5 * alive)

        @pl.loop(0, BLOCK // CHUNK)
        def _(r):
            rows = pl.ds(pl.multiple_of(r * CHUNK, CHUNK), CHUNK)
            upstream = gsum[rows, :]
            total = jnp.zeros_like(upstream)
            for k in range(fan):
                g = upstream * slope[k, rows, :].astype(F32)
                total = total + g
                gacc[ids[k], rows, :] += g
            tgrad[pl.ds(pl.multiple_of(i * BLOCK + r * CHUNK, CHUNK), CHUNK), :] = total.astype(BF)

    @pl.loop(0, block_count)
    def _(b):
        g = gacc[b].astype(BF)
        part_o[block_rows(b), :] = dot_nt(g, w1f[width:, :])
        dsrc[...] += dot_tn(feats[block_rows(b), :], g)

    @pl.loop(0, ghost_count)
    def _(b):
        g = gacc[block_count + b].astype(BF)
        ghost_o[block_rows(b), :] = dot_nt(g, w1f[width:, :]).astype(BF)
        dsrc[...] += dot_tn(ghosts[block_rows(b), :], g)

    @pl.loop(0, own)
    def _(i):
        rows = block_rows(core * own + i)
        rows_i = block_rows(i)
        part_o[rows, :] += gxnode[rows_i, :] + dot_nt(tgrad[rows_i, :], w1f[:width, :])

    own_feats = pair[:, :width]
    dtgt = dot_tn(own_feats, tgrad[...])
    dnode = dot_tn(pair[...], gnode[...])
    dew2 = dot_tn(esum[...], gmsg[...])
    dnw2 = dot_tn(hidden[...], gupd[...])
    ones = jnp.ones((16, own * BLOCK), BF)
    deb = dot_nn(ones, tgrad[...])[:1, :]
    dnb = dot_nn(ones, gnode[...])[:1, :]
    dgain_row = dgain[...].astype(BF).astype(F32)
    for out, lo in ((mine_o, 0), (other_o, quarter)):
        kind = out.dtype
        at = 0
        for c in range(lo, lo + quarter, 128):
            out[at : at + width, :] = dtgt[:, c : c + 128].astype(kind)
            out[at + width : at + 2 * width, :] = dsrc[:, c : c + 128].astype(kind)
            at += 2 * width
        for c in range(lo, lo + quarter, 128):
            out[at : at + 2 * width, :] = dnode[:, c : c + 128].astype(kind)
            at += 2 * width
        out[at : at + quarter, :] = dew2[lo : lo + quarter, :].astype(kind)
        at += quarter
        out[at : at + quarter, :] = dnw2[lo : lo + quarter, :].astype(kind)
        at += quarter
        lines = [deb[:, c : c + 128] for c in range(lo, lo + quarter, 128)]
        lines += [dnb[:, c : c + 128] for c in range(lo, lo + quarter, 128)]
        lines += [dgain_row]
        lines += [jnp.zeros((16 - len(lines), 128), F32)]
        out[at : at + 16, :] = jnp.concatenate(lines, axis=0).astype(kind)
        at += 16
        if at < out.shape[0]:
            out[at:, :] = jnp.zeros((out.shape[0] - at, 128), kind)


def reduce_kernel(dom_count, case_count, bound, *refs):
    send, part, ghost_grad, w_mine, w_other, new_mine = refs[:6]
    final, node_mine, node_other, new_other = refs[6:10]
    (
        ghost_in, twin_in, reduced, case_in, case_red, dom_in,
        twin_send, twin_recv, ghost_send, ghost_recv, case_send, case_recv,
        dom_send, dom_recv, gd_send, gd_recv, gc_send, gc_recv,
    ) = refs[10:]
    here = lax.axis_index("dom")
    case = lax.axis_index("case")
    twin = {"sub": 1 - lax.axis_index("sub")}
    span = bound * BLOCK
    total = w_mine.shape[0]
    slab = total // case_count
    piece = slab // dom_count
    block_count = part.shape[0] // BLOCK

    barrier = pltpu.get_barrier_semaphore()
    pl.semaphore_signal(barrier, inc=1, device_id=twin, device_id_type=MESH)
    for o in range(1, dom_count):
        pl.semaphore_signal(
            barrier, inc=1, device_id={"dom": lax.rem(here + o, dom_count)}, device_id_type=MESH
        )
    for o in range(1, case_count):
        pl.semaphore_signal(
            barrier, inc=1, device_id={"case": lax.rem(case + o, case_count)}, device_id_type=MESH
        )
    pl.semaphore_wait(barrier, 1 + (dom_count - 1) + (case_count - 1))

    twin_w = remote(w_other, twin_in, twin_send.at[0], twin_recv.at[0], twin)
    twin_w.start()

    def ghost_copy(j, there):
        return remote(
            ghost_grad.at[pl.ds(j * span, span)],
            ghost_in.at[pl.ds(j * span, span)],
            ghost_send.at[j],
            ghost_recv.at[j],
            {"dom": there},
        )

    for j in (2, 3, 0, 1):
        there = here - DISTANCES[j]

        @pl.when(inside(there, dom_count))
        def _():
            ghost_copy(j, there).start()

    twin_new = remote(new_mine, new_other, twin_send.at[1], twin_recv.at[1], twin)
    twin_new.start()
    for j in range(4):

        @pl.when(jnp.logical_not(inside(here + DISTANCES[j], dom_count)))
        def _():
            ghost_in[j * span : (j + 1) * span, :] = jnp.zeros((span, 128), BF)

    def slab_rows(c):
        return pl.ds(pl.multiple_of(c * slab, 16), slab)

    def piece_rows(d):
        return pl.ds(pl.multiple_of(d * piece, 16), piece)

    def final_rows(c, d):
        return pl.ds(pl.multiple_of(c * slab + d * piece, 16), piece)

    twin_w.wait()
    case_copies = []
    for o in range(1, case_count):
        peer = lax.rem(case + o, case_count)
        rows = slab_rows(peer)
        reduced[o - 1] = (w_mine[rows, :] + twin_in[rows, :].astype(F32)).astype(BF)
        copy = remote(
            reduced.at[o - 1],
            case_in.at[o - 1],
            case_send.at[o - 1],
            case_recv.at[o - 1],
            {"case": peer},
        )
        copy.start()
        case_copies.append(copy)

    for j in range(4):

        @pl.when(inside(here + DISTANCES[j], dom_count))
        def _():
            ghost_copy(j, here + DISTANCES[j]).wait_recv()

    hits = [
        [jnp.where(send[j, m] == b, 1.0, 0.0) for j in range(4) for m in range(bound)]
        for b in range(block_count)
    ]

    @pl.loop(0, BLOCK // CHUNK)
    def _(r):
        slots = [
            ghost_in[pl.ds(pl.multiple_of(s * BLOCK + r * CHUNK, CHUNK), CHUNK), :].astype(F32)
            for s in range(4 * bound)
        ]
        for b in range(block_count):
            rows = pl.ds(pl.multiple_of(b * BLOCK + r * CHUNK, CHUNK), CHUNK)
            value = part[rows, :]
            for s in range(4 * bound):
                value = value + hits[b][s] * slots[s]
            node_mine[rows, :] = value.astype(BF)

    twin_node = remote(node_mine, node_other, twin_send.at[2], twin_recv.at[2], twin)
    twin_node.start()

    for copy in case_copies:
        copy.wait()
    rows = slab_rows(case)
    value = w_mine[rows, :] + twin_in[rows, :].astype(F32)
    for o in range(1, case_count):
        value = value + case_in[o - 1].astype(F32)
    case_red[...] = value.astype(BF)
    dom_copies = []
    for o in range(1, dom_count):
        peer = lax.rem(here + o, dom_count)
        copy = remote(
            case_red.at[piece_rows(peer)],
            dom_in.at[o - 1],
            dom_send.at[o - 1],
            dom_recv.at[o - 1],
            {"dom": peer},
        )
        copy.start()
        dom_copies.append(copy)
    for copy in dom_copies:
        copy.wait()
    value = case_red[piece_rows(here), :].astype(F32)
    for o in range(1, dom_count):
        value = value + dom_in[o - 1].astype(F32)
    final[final_rows(case, here), :] = value.astype(BF)

    def dom_gather(o, owner, peer):
        rows = final_rows(case, owner)
        return remote(
            final.at[rows], final.at[rows], gd_send.at[o], gd_recv.at[o], {"dom": peer}
        )

    def case_gather(o, oz, source):
        rows = final_rows(source, lax.rem(here - oz + dom_count, dom_count))
        n = (o - 1) * dom_count + oz
        return remote(
            final.at[rows],
            final.at[rows],
            gc_send.at[n],
            gc_recv.at[n],
            {"case": lax.rem(case + o, case_count)},
        )

    for o in range(1, dom_count):
        dom_gather(o - 1, here, lax.rem(here + o, dom_count)).start()
    for oz in range(dom_count):
        if oz > 0:
            source = lax.rem(here - oz + dom_count, dom_count)
            dom_gather(oz - 1, source, source).wait_recv()
        for o in range(1, case_count):
            case_gather(o, oz, case).start()
    twin_new.wait()
    twin_node.wait()
    for j in range(4):

        @pl.when(inside(here - DISTANCES[j], dom_count))
        def _():
            ghost_copy(j, here - DISTANCES[j]).wait_send()

    for o in range(1, dom_count):
        dom_gather(o - 1, here, lax.rem(here + o, dom_count)).wait_send()
    for oz in range(dom_count):
        for o in range(1, case_count):
            case_gather(o, oz, case).wait_send()
            case_gather(o, oz, lax.rem(case - o + case_count, case_count)).wait_recv()


def unpack_kernel(final, node_mine, node_other, new_mine, new_other, *outs):
    new_nodes, node_grads, dew1, deb, dew2, dnw1, dnb, dnw2, dgain = outs
    core = lax.axis_index("sub")
    half = new_mine.shape[0]
    new_nodes[pl.ds(pl.multiple_of(core * half, BLOCK), half), :] = new_mine[...]
    new_nodes[pl.ds(pl.multiple_of((1 - core) * half, BLOCK), half), :] = new_other[...]
    node_grads[...] = (node_mine[...].astype(F32) + node_other[...].astype(F32)).astype(BF)
    at = 0
    tall = dew1.shape[0]
    quarter = dew1.shape[1]
    for out in (dew1, dnw1):
        for c in range(0, quarter, 128):
            out[:, c : c + 128] = final[at : at + tall, :].astype(F32)
            at += tall
    for out in (dew2, dnw2):
        out[...] = final[at : at + quarter, :].astype(F32)
        at += quarter
    tail = final[at : at + 16, :].astype(F32)
    n = quarter // 128
    for c in range(n):
        deb[:, c * 128 : (c + 1) * 128] = tail[c : c + 1, :]
        dnb[:, c * 128 : (c + 1) * 128] = tail[n + c : n + c + 1, :]
    dgain[...] = tail[2 * n : 2 * n + 1, :]


def on_device(
    dom_count,
    case_count,
    node_feats,
    cotangent,
    block_counts,
    neighbours,
    send_sets,
    edge_w1,
    edge_b1,
    edge_w2,
    node_w1,
    node_b1,
    node_w2,
    norm_gain,
):
    feats = node_feats[0]
    cot = cotangent[0]
    rows, width = feats.shape
    block_count, fan = neighbours.shape
    bound = send_sets.shape[1]
    quarter = edge_w1.shape[1]
    wide = 2 * quarter
    ghost_rows = 4 * bound * BLOCK
    ext_count = block_count + 4 * bound
    half = rows // 2
    vmem = pl.BlockSpec(memory_space=pltpu.VMEM)
    smem = pl.BlockSpec(memory_space=pltpu.SMEM)
    shape = jax.ShapeDtypeStruct
    dma = pltpu.SemaphoreType.DMA
    eb = edge_b1.reshape(1, quarter)
    nb = node_b1.reshape(1, quarter)
    gain = norm_gain.reshape(1, width)
    mine = (edge_w1, eb, edge_w2, node_w1, nb, node_w2)

    gathered = pl.pallas_call(
        functools.partial(gather_kernel, dom_count, bound),
        out_shape=[shape((ghost_rows, width), BF)] + [shape(m.shape, m.dtype) for m in mine],
        in_specs=[smem] + [vmem] * 7,
        out_specs=[vmem] * 7,
        scratch_shapes=[
            pltpu.VMEM((4, bound * BLOCK, width), BF),
            dma((6,)),
            dma((6,)),
            dma((4,)),
            dma((4,)),
        ],
        compiler_params=pltpu.CompilerParams(
            collective_id=0, has_side_effects=True, vmem_limit_bytes=16 << 20
        ),
        name="gather",
    )(send_sets, feats.reshape(block_count, BLOCK, width), *mine)
    ghosts = gathered[0]
    weights = []
    for m, other in zip(mine, gathered[1:]):
        weights += [m, other]

    own_rows = 6 * quarter + 16
    unit = 16 * dom_count * case_count
    total = -(-own_rows // unit) * unit
    slab = total // case_count
    piece = slab // dom_count

    new_mine, part, ghost_grad, w_mine, w_other = pl.pallas_call(
        layer_kernel,
        out_shape=[
            shape((half, width), BF),
            shape((rows, width), F32),
            shape((ghost_rows, width), BF),
            shape((total, 128), F32),
            shape((total, 128), BF),
        ],
        in_specs=[smem, smem] + [vmem] * 16,
        out_specs=[vmem] * 5,
        scratch_shapes=[
            pltpu.VMEM((2 * width, wide), BF),
            pltpu.VMEM((2 * width, wide), BF),
            pltpu.VMEM((wide, width), BF),
            pltpu.VMEM((2 * width, wide), BF),
            pltpu.VMEM((wide, width), BF),
            pltpu.VMEM((ext_count, BLOCK, wide), F32),
            pltpu.VMEM((BLOCK, wide), F32),
            pltpu.VMEM((fan, BLOCK, wide), BF),
            pltpu.VMEM((ext_count, BLOCK, wide), F32),
            pltpu.VMEM((BLOCK, wide), F32),
            pltpu.VMEM((half, wide), BF),
            pltpu.VMEM((half, 2 * width), BF),
            pltpu.VMEM((half, wide), BF),
            pltpu.VMEM((half, width), BF),
            pltpu.VMEM((half, wide), BF),
            pltpu.VMEM((half, width), BF),
            pltpu.VMEM((half, wide), BF),
            pltpu.VMEM((half, width), F32),
            pltpu.VMEM((width, wide), F32),
            pltpu.VMEM((1, width), F32),
        ],
        compiler_params=pltpu.CompilerParams(vmem_limit_bytes=40 << 20),
        name="layer",
    )(block_counts, neighbours, feats, cot, ghosts, *weights, gain)

    final, node_mine, node_other, new_other = pl.pallas_call(
        functools.partial(reduce_kernel, dom_count, case_count, bound),
        out_shape=[
            shape((total, 128), BF),
            shape((rows, width), BF),
            shape((rows, width), BF),
            shape((half, width), BF),
        ],
        in_specs=[smem] + [vmem] * 5,
        out_specs=[vmem] * 4,
        scratch_shapes=[
            pltpu.VMEM((ghost_rows, width), BF),
            pltpu.VMEM((total, 128), BF),
            pltpu.VMEM((case_count - 1, slab, 128), BF),
            pltpu.VMEM((case_count - 1, slab, 128), BF),
            pltpu.VMEM((slab, 128), BF),
            pltpu.VMEM((dom_count - 1, piece, 128), BF),
            dma((3,)),
            dma((3,)),
            dma((4,)),
            dma((4,)),
            dma((case_count - 1,)),
            dma((case_count - 1,)),
            dma((dom_count - 1,)),
            dma((dom_count - 1,)),
            dma((dom_count - 1,)),
            dma((dom_count - 1,)),
            dma(((case_count - 1) * dom_count,)),
            dma(((case_count - 1) * dom_count,)),
        ],
        compiler_params=pltpu.CompilerParams(
            collective_id=1, has_side_effects=True, vmem_limit_bytes=24 << 20
        ),
        name="reduce",
    )(send_sets, part, ghost_grad, w_mine, w_other, new_mine)

    outs = pl.pallas_call(
        unpack_kernel,
        out_shape=[
            shape((rows, width), BF),
            shape((rows, width), BF),
            shape((2 * width, quarter), F32),
            shape((1, quarter), F32),
            shape((quarter, width), F32),
            shape((2 * width, quarter), F32),
            shape((1, quarter), F32),
            shape((quarter, width), F32),
            shape((1, width), F32),
        ],
        in_specs=[vmem] * 5,
        out_specs=[vmem] * 9,
        compiler_params=pltpu.CompilerParams(vmem_limit_bytes=16 << 20),
        name="unpack",
    )(final, node_mine, node_other, new_mine, new_other)
    return (
        outs[0][None],
        outs[1][None],
        outs[2],
        outs[3].reshape(quarter),
        outs[4],
        outs[5],
        outs[6].reshape(quarter),
        outs[7],
        outs[8].reshape(width),
    )


def solution(mesh):
    placed = (
        P(("groups", "case"), "dom", None),
        P(("groups", "case"), "dom", None),
        P(("groups", "dom")),
        P(("groups", "dom"), None),
        P(("groups", "dom"), None),
        P(None, "sub"),
        P("sub"),
        P("sub", None),
        P(None, "sub"),
        P("sub"),
        P("sub", None),
        P(),
    )
    return jax.shard_map(
        functools.partial(on_device, mesh.shape["dom"], mesh.shape["case"]),
        mesh=mesh,
        in_specs=placed,
        out_specs=(
            P(("groups", "case"), "dom", None),
            P(("groups", "case"), "dom", None),
            P("groups", "sub"),
            P(("groups", "sub")),
            P(("groups", "sub"), None),
            P("groups", "sub"),
            P(("groups", "sub")),
            P(("groups", "sub"), None),
            P("groups"),
        ),
        check_vma=False,
    )
```

time: 295 us -> 69.7 us (0.24)
  waiting for transfers between devices: 95.6 us -> 0 us
  matrix products: 62.6 us -> 0 us
  Pallas kernels: 0 us -> 60.3 us
  blocking collectives: 33.5 us -> 0 us
  local copies, waits for them, and re-layouts: 38.8 us -> 7.52 us
  starting transfers between devices: 24.1 us -> 0 us
  other arithmetic: 23.1 us -> 0 us
  between operations: 15 us -> 1.39 us
    psum x3 -> x0, waiting for transfers between devices: 93.5 us -> none  [the longest x1 72.1 us: on_device(): lax.psum((d_edge_w1, d_edge_b1, d_edge_w2, d_node_w1, d_node_b1, d_node_w...]
    dot_general x54 -> x0, matrix products: 62.6 us -> none  [the longest x10 18.5 us: edge_preact(): jnp.dot(sources.reshape(-1, feat_width), source_w1, preferred_element_typ...]
    pallas_call x0 -> x4, Pallas kernels: none -> 60.3 us  [the longest x1 26.2 us: on_device(): pl.pallas_call(functools.partial(reduce_kernel, dom_count, case_count, bo...]
    psum x3 -> x0, blocking collectives: 33.5 us -> none  [the longest x1 23.1 us: on_device(): lax.psum((d_edge_w1, d_edge_b1, d_edge_w2, d_node_w1, d_node_b1, d_node_w...]
    ppermute x8 -> x0, starting transfers between devices: 24 us -> none  [passed_along(): return lax.ppermute(block, axis, route)]
    gather x14 -> x0, local copies, waits for them, and re-layouts: 12.6 us -> none  [the longest x10 6.48 us: edge_preact(): sources = extended[jnp.maximum(link_ids, 0).reshape(-1)]]
    gt x10 -> x0, other arithmetic: 6.93 us -> none  [mask_edges(): present = (link_ids >= 0) & (alive_rows[:, None] > 0)]
    reduce_sum x4 -> x0, other arithmetic: 5.82 us -> none  [the longest x1 1.81 us: normalize(): shifted = values - centre]
  transfers between devices with their start and end apart: 11 -> 0, of which waited for: 4 -> 0; matrix products, arithmetic and copies ran while one was open for 6% -> 0% of each run, Pallas kernels for 0% -> 0%
where the time goes in v1:
time: 69.7 us; the launch traced here: 69.2 us
  Pallas kernels  60.3 us (87%)
  local copies, waits for them, and re-layouts  7.52 us (11%)
  between operations  1.39 us (2%)
    pallas_call x1, Pallas kernels, on_device(): pl.pallas_call(functools.partial(reduce_kernel, dom_count, case_count, bo...  26.2 us
    pallas_call x1, Pallas kernels, on_device(): pl.pallas_call(layer_kernel, out_shape=[shape((half, width), BF), shape((...  22.8 us
    pallas_call x1, Pallas kernels, on_device(): pl.pallas_call(functools.partial(gather_kernel, dom_count, bound), out_sh...  10.1 us
    unnamed x34, local copies, waits for them, and re-layouts  7.52 us

profile of v1, /device:TPU:0, one launch (start us, length us, event | category | flops | bytes accessed | tf_op | source)
XLA Modules:
  0.0 69.2 jit_solution(16950610479348775765)
XLA Ops:
  1.3 0.0 copy-start.14
  1.3 0.7 copy-done.15
  2.0 0.1 copy.23.refs_0_
  2.1 0.0 copy-done.14
  2.1 0.1 copy.22.links
  2.2 0.6 copy-done.11
  2.8 0.0 copy-done.12
  2.8 1.0 %copy-done = bf16[1,1280,128]{2,1,0:T(8,128)(2,1)S(1)} copy-done((bf16[1,1280,128]{2,1,0:T(8,128)(2,1)S(1)}, bf16[1,1280,128]{2,1,0:T(8,128)(2,1)}, u32[]{:S(2)}) %copy-start) | copy-done | bytes 327704
  3.8 0.9 %copy-done.2 = bf16[256,256]{1,0:T(8,128)(2,1)S(1)} copy-done((bf16[256,256]{1,0:T(8,128)(2,1)S(1)}, bf16[256,256]{1,0:T(8,128)(2,1)}, u32[]{:S(2)}) %copy-start.2) | copy-done | bytes 131096
  4.7 0.9 %copy-done.4 = bf16[256,256]{1,0:T(8,128)(2,1)S(1)} copy-done((bf16[256,256]{1,0:T(8,128)(2,1)S(1)}, bf16[256,256]{1,0:T(8,128)(2,1)}, u32[]{:S(2)}) %copy-start.4) | copy-done | bytes 131096
  5.6 0.8 %copy-done.7 = bf16[256,128]{1,0:T(8,128)(2,1)S(1)} copy-done((bf16[256,128]{1,0:T(8,128)(2,1)S(1)}, bf16[256,128]{1,0:T(8,128)(2,1)}, u32[]{:S(2)}) %copy-start.7) | copy-done | bytes 65560
  6.4 0.8 %copy-done.9 = bf16[256,128]{1,0:T(8,128)(2,1)S(1)} copy-done((bf16[256,128]{1,0:T(8,128)(2,1)S(1)}, bf16[256,128]{1,0:T(8,128)(2,1)}, u32[]{:S(2)}) %copy-start.9) | copy-done | bytes 65560
  7.3 10.1 %gather.1 = (bf16[1024,128]{1,0:T(8,128)(2,1)S(1)}, bf16[256,256]{1,0:T(8,128)(2,1)S(1)}, f32[1,256]{1,0:T(1,128)S(1)}, bf16[256,128]{1,0:T(8,128)(2,1)S(1)}, bf...) custom-call(s32[4,2]{1,0:T(4,128)S(1)} %copy.23.refs_0_, ...), custom_call_target="tpu_custom_call" | custom-call | tf_op jit(solution)/shard_map/gather/pallas_call | solution.py:506
  17.4 0.0 copy-start.13
  17.4 0.0 copy-done.1
  17.4 0.0 copy-done.3
  17.4 0.0 copy-done.5
  17.4 0.0 copy-done.8
  17.4 0.0 copy-done.10
  17.4 0.6 copy-done.13
  18.0 1.0 %copy-done.6 = bf16[1,1280,128]{2,1,0:T(8,128)(2,1)S(1)} copy-done((bf16[1,1280,128]{2,1,0:T(8,128)(2,1)S(1)}, bf16[1,1280,128]{2,1,0:T(8,128)(2,1)}, u32[]{:S(2)}) %copy-start.6) | copy-done | bytes 327704
  19.0 22.8 %layer.1 = (bf16[640,128]{1,0:T(8,128)(2,1)S(1)}, f32[1280,128]{1,0:T(8,128)S(1)}, bf16[1024,128]{1,0:T(8,128)(2,1)S(1)}, f32[1664,128]{1,0:T(8,128)S(1)}, bf16[1664,128]{1,0:T(8,128)(2,1)S(1)}) custom-call(s32[1]{0:T(128)S(6)} %copy.24.counts, s32[10,8]{1,0:T(8,128)S(1)} %copy.22.links, bf16[1280,128]{1,0:T(8,128)(2,1)S(1)} %bitcast.12, ...), custom_call_target="tpu_custom_call" | custom-call | tf_op jit(solution)/shard_map/layer/pallas_call | solution.py:534
  41.8 26.2 %reduce.1 = (bf16[1664,128]{1,0:T(8,128)(2,1)S(1)}, bf16[1280,128]{1,0:T(8,128)(2,1)S(1)}, bf16[1280,128]{1,0:T(8,128)(2,1)S(1)}, bf16[640,128]{1,0:T(8,128)(2,1)S(1)}) custom-call(s32[4,2]{1,0:T(4,128)S(1)} %copy.23.refs_0_, f32[1280,128]{1,0:T(8,128)S(1)} %get-tuple-element.41.refs_1_, bf16[1024,128]{1,0:T(8,128)(2,1)S(1)} %get-tuple-element.42.refs_2_, ...), custom_call_target="tpu_custom_call" | custom-call | tf_op jit(solution)/shard_map/reduce/pallas_call | solution.py:571
  68.1 1.2 %unpack.1 = (bf16[1280,128]{1,0:T(8,128)(2,1)}, bf16[1280,128]{1,0:T(8,128)(2,1)}, f32[256,256]{1,0:T(8,128)}, f32[1,256]{1,0:T(1,128)}, f32[256,128]{1,0:T(8,12...) custom-call(bf16[1664,128]{1,0:T(8,128)(2,1)S(1)} %get-tuple-element.46.final, ...), custom_call_target="tpu_custom_call" | custom-call | tf_op jit(solution)/shard_map/unpack/pallas_call | solution.py:607
  (14 shorter events, 0.0 us)
Async XLA Ops:
  1.3 0.8 %copy-start.14 = (s32[10,8]{0,1:T(8,128)S(1)}, s32[10,8]{0,1:T(8,128)}, u32[]{:S(2)}) copy-start(s32[10,8]{0,1:T(8,128)} %param.15) | copy-start | bytes 964
  1.3 0.7 copy-start.15
  2.1 0.7 copy-start.11
  2.1 0.7 %copy-start.12 = (f32[256]{0:T(256)S(1)}, f32[256]{0:T(256)}, u32[]{:S(2)}) copy-start(f32[256]{0:T(256)} %param.21) | copy-start | bytes 3076
  2.8 1.0 %copy-start = (bf16[1,1280,128]{2,1,0:T(8,128)(2,1)S(1)}, bf16[1,1280,128]{2,1,0:T(8,128)(2,1)}, u32[]{:S(2)}) copy-start(bf16[1,1280,128]{2,1,0:T(8,128)(2,1)} %param.12) | copy-start | bytes 983044
  3.7 0.9 %copy-start.2 = (bf16[256,256]{1,0:T(8,128)(2,1)S(1)}, bf16[256,256]{1,0:T(8,128)(2,1)}, u32[]{:S(2)}) copy-start(bf16[256,256]{1,0:T(8,128)(2,1)} %refs_0_.3) | copy-start | bytes 393220
  4.7 0.9 %copy-start.4 = (bf16[256,256]{1,0:T(8,128)(2,1)S(1)}, bf16[256,256]{1,0:T(8,128)(2,1)}, u32[]{:S(2)}) copy-start(bf16[256,256]{1,0:T(8,128)(2,1)} %refs_6_.1) | copy-start | bytes 393220
  5.6 0.8 %copy-start.7 = (bf16[256,128]{1,0:T(8,128)(2,1)S(1)}, bf16[256,128]{1,0:T(8,128)(2,1)}, u32[]{:S(2)}) copy-start(bf16[256,128]{1,0:T(8,128)(2,1)} %refs_4_.3) | copy-start | bytes 196612
  6.4 0.8 %copy-start.9 = (bf16[256,128]{1,0:T(8,128)(2,1)S(1)}, bf16[256,128]{1,0:T(8,128)(2,1)}, u32[]{:S(2)}) copy-start(bf16[256,128]{1,0:T(8,128)(2,1)} %refs_10_.1) | copy-start | bytes 196612
  7.2 10.2 %copy-start.1 = (bf16[1,1280,128]{2,1,0:T(8,128)(2,1)S(1)}, bf16[1,1280,128]{2,1,0:T(8,128)(2,1)}, u32[]{:S(2)}) copy-start(bf16[1,1280,128]{2,1,0:T(8,128)(2,1)} %param.12) | copy-start | bytes 983044
  7.2 10.2 %copy-start.3 = (bf16[256,256]{1,0:T(8,128)(2,1)S(1)}, bf16[256,256]{1,0:T(8,128)(2,1)}, u32[]{:S(2)}) copy-start(bf16[256,256]{1,0:T(8,128)(2,1)} %refs_0_.3) | copy-start | bytes 393220
  7.2 10.2 %copy-start.5 = (bf16[256,256]{1,0:T(8,128)(2,1)S(1)}, bf16[256,256]{1,0:T(8,128)(2,1)}, u32[]{:S(2)}) copy-start(bf16[256,256]{1,0:T(8,128)(2,1)} %refs_6_.1) | copy-start | bytes 393220
  7.2 10.2 %copy-start.8 = (bf16[256,128]{1,0:T(8,128)(2,1)S(1)}, bf16[256,128]{1,0:T(8,128)(2,1)}, u32[]{:S(2)}) copy-start(bf16[256,128]{1,0:T(8,128)(2,1)} %refs_4_.3) | copy-start | bytes 196612
  7.2 10.2 %copy-start.10 = (bf16[256,128]{1,0:T(8,128)(2,1)S(1)}, bf16[256,128]{1,0:T(8,128)(2,1)}, u32[]{:S(2)}) copy-start(bf16[256,128]{1,0:T(8,128)(2,1)} %refs_10_.1) | copy-start | bytes 196612
  17.4 0.7 copy-start.13
  18.0 1.0 %copy-start.6 = (bf16[1,1280,128]{2,1,0:T(8,128)(2,1)S(1)}, bf16[1,1280,128]{2,1,0:T(8,128)(2,1)}, u32[]{:S(2)}) copy-start(bf16[1,1280,128]{2,1,0:T(8,128)(2,1)} %param.13) | copy-start | bytes 983044

commit v2 on v1

v2 whole, which is shorter than its diff:
```python
import functools

import jax
import jax.numpy as jnp
from jax import lax
from jax.experimental import pallas as pl
from jax.experimental.pallas import tpu as pltpu
from jax.sharding import PartitionSpec as P

BLOCK = 128
CHUNK = 16
DISTANCES = (1, -1, 2, -2)
EPSILON = 1e-05
MESH = pl.DeviceIdType.MESH
BF = jnp.bfloat16
F32 = jnp.float32


def dot_nn(a, b):
    return lax.dot_general(a, b, (((1,), (0,)), ((), ())), preferred_element_type=F32)


def dot_nt(a, b):
    return lax.dot_general(a, b, (((1,), (1,)), ((), ())), preferred_element_type=F32)


def dot_tn(a, b):
    return lax.dot_general(a, b, (((0,), (0,)), ((), ())), preferred_element_type=F32)


def inside(position, count):
    return (position >= 0) & (position < count)


def remote(src, dst, send_sem, recv_sem, device):
    return pltpu.make_async_remote_copy(
        src_ref=src,
        dst_ref=dst,
        send_sem=send_sem,
        recv_sem=recv_sem,
        device_id=device,
        device_id_type=MESH,
    )


def chain_kernel(links, prev_o, last_o):
    core = lax.axis_index("sub")
    block_count, fan = links.shape
    own = block_count // 2
    none = own * fan

    @pl.loop(0, last_o.shape[0])
    def _(s):
        last_o[s] = none

    @pl.loop(0, none)
    def _(e):
        source = jnp.maximum(links[core * own + e // fan, lax.rem(e, fan)], 0)
        prev_o[e] = last_o[source]
        last_o[source] = e


class Reducer:
    def __init__(self, dom_count, case_count, final, refs):
        (self.mine, self.other, self.twin_in, self.reduced, self.case_in, self.case_red,
         self.dom_in, self.send, self.recv) = refs
        self.final = final
        self.dom_count, self.case_count = dom_count, case_count
        self.here, self.case = lax.axis_index("dom"), lax.axis_index("case")
        self.twin = {"sub": 1 - lax.axis_index("sub")}
        self.slab = self.mine.shape[0] // case_count
        self.piece = self.slab // dom_count

    def copy(self, src, dst, n, device):
        return remote(src, dst, self.send.at[n], self.recv.at[n], device)

    def slab_rows(self, c):
        return pl.ds(pl.multiple_of(c * self.slab, 16), self.slab)

    def piece_rows(self, d):
        return pl.ds(pl.multiple_of(d * self.piece, 16), self.piece)

    def final_rows(self, c, d):
        return pl.ds(pl.multiple_of(c * self.slab + d * self.piece, 16), self.piece)

    def case_peer(self, o):
        return lax.rem(self.case + o, self.case_count)

    def dom_peer(self, o):
        return lax.rem(self.here + o, self.dom_count)

    def sub_copy(self):
        return self.copy(self.other, self.twin_in, 0, self.twin)

    def case_copy(self, o):
        return self.copy(
            self.reduced.at[o - 1], self.case_in.at[o - 1], o, {"case": self.case_peer(o)}
        )

    def dom_copy(self, o):
        peer = self.dom_peer(o)
        return self.copy(
            self.case_red.at[self.piece_rows(peer)],
            self.dom_in.at[o - 1],
            self.case_count + o - 1,
            {"dom": peer},
        )

    def dom_gather(self, o, owner, peer):
        rows = self.final_rows(self.case, owner)
        n = self.case_count + self.dom_count - 1 + o - 1
        return self.copy(self.final.at[rows], self.final.at[rows], n, {"dom": peer})

    def case_gather(self, o, oz, source):
        owner = lax.rem(self.here - oz + self.dom_count, self.dom_count)
        rows = self.final_rows(source, owner)
        n = self.case_count + 2 * (self.dom_count - 1) + (o - 1) * self.dom_count + oz
        return self.copy(
            self.final.at[rows], self.final.at[rows], n, {"case": self.case_peer(o)}
        )

    def to_sub(self):
        self.sub_copy().start()

    def to_case(self):
        self.sub_copy().wait()
        for o in range(1, self.case_count):
            rows = self.slab_rows(self.case_peer(o))
            self.reduced[o - 1] = (self.mine[rows, :] + self.twin_in[rows, :].astype(F32)).astype(BF)
            self.case_copy(o).start()

    def to_dom(self):
        for o in range(1, self.case_count):
            self.case_copy(o).wait()
        rows = self.slab_rows(self.case)
        value = self.mine[rows, :] + self.twin_in[rows, :].astype(F32)
        for o in range(1, self.case_count):
            value = value + self.case_in[o - 1].astype(F32)
        self.case_red[...] = value.astype(BF)
        for o in range(1, self.dom_count):
            self.dom_copy(o).start()

    def to_gather(self):
        for o in range(1, self.dom_count):
            self.dom_copy(o).wait()
        value = self.case_red[self.piece_rows(self.here), :].astype(F32)
        for o in range(1, self.dom_count):
            value = value + self.dom_in[o - 1].astype(F32)
        self.final[self.final_rows(self.case, self.here), :] = value.astype(BF)
        for o in range(1, self.dom_count):
            self.dom_gather(o, self.here, self.dom_peer(o)).start()
        for o in range(1, self.case_count):
            self.case_gather(o, 0, self.case).start()

    def forward(self):
        for oz in range(1, self.dom_count):
            source = lax.rem(self.here - oz + self.dom_count, self.dom_count)
            self.dom_gather(oz, source, source).wait_recv()
            for o in range(1, self.case_count):
                self.case_gather(o, oz, self.case).start()

    def finish(self):
        for o in range(1, self.dom_count):
            self.dom_gather(o, self.here, self.dom_peer(o)).wait_send()
        for oz in range(self.dom_count):
            for o in range(1, self.case_count):
                self.case_gather(o, oz, self.case).wait_send()
                source = lax.rem(self.case - o + self.case_count, self.case_count)
                self.case_gather(o, oz, source).wait_recv()


def fill(out, pieces, lines):
    at = 0
    for piece in pieces:
        out[at : at + piece.shape[0], :] = piece.astype(out.dtype)
        at += piece.shape[0]
    lines = lines + [jnp.zeros((16 - len(lines), 128), F32)]
    out[at : at + 16, :] = jnp.concatenate(lines, axis=0).astype(out.dtype)
    at += 16
    if at < out.shape[0]:
        out[at:, :] = jnp.zeros((out.shape[0] - at, 128), out.dtype)


def columns(value, lo, hi):
    return [value[:, c : c + 128] for c in range(lo, hi, 128)]


def layer_kernel(dom_count, case_count, bound, *refs):
    send, counts, links, prev, last = refs[:5]
    feats_h, cot_h, gain_h = refs[5:8]
    mine = refs[8:14]
    final_n, final_e, node_mine, node_other, new_mine, new_other = refs[14:20]
    reducer_n = Reducer(dom_count, case_count, final_n, refs[20:29])
    reducer_e = Reducer(dom_count, case_count, final_e, refs[29:38])
    (
        feats, cot, gain, stage, ghosts, ext,
        w1f, ebias, w2f, n1f, nbias, n2f, w1h,
        psrc, ptgt, slope, gsum, esum, pair, hidden, gupd, gnode,
        gmsg, tgrad, gxnode, dsrc, dgain, srcs, chain, ghost_grad, ghost_in,
        local, half_send, half_recv, ghost_send, ghost_recv, home_send, home_recv,
        twin_send, twin_recv,
    ) = refs[38:]
    core = lax.axis_index("sub")
    here = lax.axis_index("dom")
    case = lax.axis_index("case")
    twin = {"sub": 1 - core}
    block_count, fan = links.shape
    width = feats.shape[2]
    quarter = mine[0].shape[1]
    wide = 2 * quarter
    own = block_count // 2
    ghost_count = 4 * bound
    none = own * fan
    left, right = pl.ds(0, quarter), pl.ds(quarter, quarter)

    def block_rows(b):
        return pl.ds(pl.multiple_of(b * BLOCK, BLOCK), BLOCK)

    def half_of(n, part):
        ref = (w1f, ebias, w2f, n1f, nbias, n2f)[n]
        return ref.at[part, :] if n in (2, 5) else ref.at[:, part]

    locals_ = [pltpu.make_async_copy(feats_h, feats, local.at[0])]
    locals_ += [pltpu.make_async_copy(mine[n], half_of(n, left), local.at[1 + n]) for n in range(6)]
    locals_ += [
        pltpu.make_async_copy(gain_h, gain, local.at[7]),
        pltpu.make_async_copy(cot_h, cot, local.at[8]),
    ]
    for copy in locals_:
        copy.start()

    barrier = pltpu.get_barrier_semaphore()
    pl.semaphore_signal(barrier, inc=1, device_id=twin, device_id_type=MESH)
    for o in range(1, dom_count):
        pl.semaphore_signal(
            barrier, inc=1, device_id={"dom": lax.rem(here + o, dom_count)}, device_id_type=MESH
        )
    for o in range(1, case_count):
        pl.semaphore_signal(
            barrier, inc=1, device_id={"case": lax.rem(case + o, case_count)}, device_id_type=MESH
        )
    locals_[0].wait()
    for j in range(4):
        for m in range(bound):
            stage[j, m] = feats[send[j, m]]
    pl.semaphore_wait(barrier, 1 + (dom_count - 1) + (case_count - 1))

    halves = [
        remote(mine[n], half_of(n, right), half_send.at[n], half_recv.at[n], twin)
        for n in range(6)
    ]
    halves[0].start()

    def ghost_copy(j, there):
        return remote(
            stage.at[j], ghosts.at[j], ghost_send.at[j], ghost_recv.at[j], {"dom": there}
        )

    for j in (2, 3, 0, 1):

        @pl.when(inside(here + DISTANCES[j], dom_count))
        def _():
            ghost_copy(j, here + DISTANCES[j]).start()

    for copy in halves[1:]:
        copy.start()
    for j in range(4):

        @pl.when(jnp.logical_not(inside(here - DISTANCES[j], dom_count)))
        def _():
            ghosts[j] = jnp.zeros(ghosts.shape[1:], BF)

        @pl.when(jnp.logical_not(inside(here + DISTANCES[j], dom_count)))
        def _():
            ghost_in[j] = jnp.zeros(ghost_in.shape[1:], BF)

    dgain[...] = jnp.zeros_like(dgain)
    dsrc[...] = jnp.zeros_like(dsrc)
    chain[none] = jnp.zeros(chain.shape[1:], F32)
    for copy in locals_[1:]:
        copy.wait()
    halves[0].wait()
    w1h[...] = w1f[...] * jnp.asarray(0.5, BF)

    @pl.loop(0, block_count)
    def _(b):
        ext[b] = feats[b]
        psrc[b] = dot_nn(feats[b], w1h[width:, :])

    for copy in halves[1:]:
        copy.wait()
    edge_bias = ebias[...] * 0.5
    node_bias = nbias[...]
    gain_row = gain[...]
    for j in range(4):

        @pl.when(inside(here - DISTANCES[j], dom_count))
        def _():
            ghost_copy(j, here - DISTANCES[j]).wait_recv()

        @pl.when(inside(here + DISTANCES[j], dom_count))
        def _():
            ghost_copy(j, here + DISTANCES[j]).wait_send()

        for m in range(bound):
            s = block_count + j * bound + m
            ext[s] = ghosts[j, m]
            psrc[s] = dot_nn(ghosts[j, m], w1h[width:, :])

    @pl.loop(0, own)
    def _(i):
        b = core * own + i
        alive = jnp.where(b < counts[0], 1.0, 0.0)
        ids = [jnp.maximum(links[b, k], 0) for k in range(fan)]
        rows_i = block_rows(i)
        targets = feats[b]
        ptgt[...] = dot_nn(targets, w1h[:width, :]) + edge_bias

        @pl.loop(0, BLOCK // CHUNK)
        def _(r):
            rows = pl.ds(pl.multiple_of(r * CHUNK, CHUNK), CHUNK)
            base = ptgt[rows, :]
            total = jnp.zeros_like(base)
            for k in range(fan):
                h = psrc[ids[k], rows, :] + base
                t = jnp.tanh(h)
                a = 1.0 + t
                q = h * a
                total = total + q
                at = pl.multiple_of((i * fan + k) * BLOCK + r * CHUNK, CHUNK)
                slope[pl.ds(at, CHUNK), :] = (a + q * (1.0 - t)).astype(BF)
            esum[pl.ds(pl.multiple_of(i * BLOCK + r * CHUNK, CHUNK), CHUNK), :] = (
                total * alive
            ).astype(BF)

        message = dot_nn(esum[rows_i, :], w2f[...]).astype(BF)
        pair[rows_i, :width] = targets
        pair[rows_i, width:] = message
        h = (dot_nn(pair[rows_i, :], n1f[...]) + node_bias) * 0.5
        t = jnp.tanh(h)
        a = 1.0 + t
        q = h * a
        node_slope = 0.5 * (a + q * (1.0 - t))
        hidden[rows_i, :] = q.astype(BF)
        update = dot_nn(hidden[rows_i, :], n2f[...])
        shifted = update - jnp.mean(update, axis=-1, keepdims=True)
        spread = jnp.mean(shifted * shifted, axis=-1, keepdims=True)
        scale = lax.rsqrt(spread + EPSILON)
        unit = shifted * scale
        new_mine[rows_i, :] = (targets.astype(F32) + alive * (unit * gain_row)).astype(BF)
        seed = cot[b].astype(F32) * alive
        dgain[...] += jnp.sum(seed * unit, axis=0, keepdims=True)
        seed = seed * gain_row
        grad = scale * (
            seed
            - jnp.mean(seed, axis=-1, keepdims=True)
            - unit * jnp.mean(seed * unit, axis=-1, keepdims=True)
        )
        gupd[rows_i, :] = grad.astype(BF)
        gnode[rows_i, :] = (dot_nt(gupd[rows_i, :], n2f[...]) * node_slope).astype(BF)
        back = dot_nt(gnode[rows_i, :], n1f[...])
        gxnode[rows_i, :] = back[:, :width] + cot[b].astype(F32)
        gmsg[rows_i, :] = back[:, width:].astype(BF)
        gsum[rows_i, :] = dot_nt(gmsg[rows_i, :], w2f[...]) * (0.5 * alive)

    twin_new = remote(new_mine, new_other, twin_send.at[0], twin_recv.at[0], twin)
    twin_new.start()
    ones = jnp.ones((16, own * BLOCK), BF)
    dnode = dot_tn(pair[...], gnode[...])
    dew2 = dot_tn(esum[...], gmsg[...])
    dnw2 = dot_tn(hidden[...], gupd[...])
    dnb = dot_nn(ones, gnode[...])[:1, :]
    dgain_row = dgain[...].astype(BF).astype(F32)
    for out, lo in ((reducer_n.mine, 0), (reducer_n.other, quarter)):
        hi = lo + quarter
        fill(
            out,
            columns(dnode, lo, hi) + [dew2[lo:hi, :], dnw2[lo:hi, :]],
            columns(dnb, lo, hi) + [dgain_row],
        )
    reducer_n.to_sub()

    def backward(i):
        b = core * own + i
        ids = [jnp.maximum(links[b, k], 0) for k in range(fan)]
        for k in range(fan):
            srcs[k * BLOCK : (k + 1) * BLOCK, :] = ext[ids[k]]

        @pl.loop(0, BLOCK // CHUNK)
        def _(r):
            rows = pl.ds(pl.multiple_of(i * BLOCK + r * CHUNK, CHUNK), CHUNK)
            upstream = gsum[rows, :]
            total = jnp.zeros_like(upstream)
            for k in range(fan):
                at = pl.ds(pl.multiple_of((i * fan + k) * BLOCK + r * CHUNK, CHUNK), CHUNK)
                g = upstream * slope[at, :].astype(F32)
                total = total + g
                slope[at, :] = g.astype(BF)
            tgrad[rows, :] = total.astype(BF)

        rows = pl.ds(pl.multiple_of(i * fan * BLOCK, BLOCK), fan * BLOCK)
        g = slope[rows, :]
        spread = dot_nt(g, w1f[width:, :])
        for k in range(fan):
            e = i * fan + k
            chain[e] = spread[k * BLOCK : (k + 1) * BLOCK, :] + chain[prev[e]]
        dsrc[...] += dot_tn(srcs[...], g)

    steps = [reducer_n.to_case, reducer_n.to_dom, reducer_n.to_gather, reducer_n.forward]
    for n, step in enumerate(steps):
        pl.loop(min(n, own), min(n + 1, own))(backward)
        step()
    pl.loop(min(len(steps), own), own)(backward)

    def home_copy(j, there):
        return remote(
            ghost_grad.at[j], ghost_in.at[j], home_send.at[j], home_recv.at[j], {"dom": there}
        )

    for j in (2, 3, 0, 1):
        for m in range(bound):
            ghost_grad[j, m] = chain[last[block_count + j * bound + m]].astype(BF)

        @pl.when(inside(here - DISTANCES[j], dom_count))
        def _():
            home_copy(j, here - DISTANCES[j]).start()

    dtgt = dot_tn(pair[:, :width], tgrad[...])
    deb = dot_nn(ones, tgrad[...])[:1, :]
    for out, lo in ((reducer_e.other, quarter), (reducer_e.mine, 0)):
        hi = lo + quarter
        both = zip(columns(dtgt, lo, hi), columns(dsrc[...], lo, hi))
        fill(out, [x for pieces in both for x in pieces], columns(deb, lo, hi))
        if lo > 0:
            reducer_e.to_sub()
    reducer_e.to_case()
    reducer_n.finish()

    part = psrc
    @pl.loop(0, block_count)
    def _(b):
        part[b, :, :width] = chain[last[b]]

    @pl.loop(0, own)
    def _(i):
        rows = block_rows(i)
        part[core * own + i, :, :width] += gxnode[rows, :] + dot_nt(tgrad[rows, :], w1f[:width, :])

    for j in range(4):

        @pl.when(inside(here + DISTANCES[j], dom_count))
        def _():
            home_copy(j, here + DISTANCES[j]).wait_recv()

    reducer_e.to_dom()
    hits = [
        [jnp.where(send[j, m] == b, 1.0, 0.0) for j in range(4) for m in range(bound)]
        for b in range(block_count)
    ]

    @pl.loop(0, BLOCK // CHUNK)
    def _(r):
        rows = pl.ds(pl.multiple_of(r * CHUNK, CHUNK), CHUNK)
        slots = [
            ghost_in[j, m, rows, :].astype(F32) for j in range(4) for m in range(bound)
        ]
        for b in range(block_count):
            value = part[b, rows, :width]
            for s in range(ghost_count):
                value = value + hits[b][s] * slots[s]
            node_mine[pl.ds(pl.multiple_of(b * BLOCK + r * CHUNK, CHUNK), CHUNK), :] = (
                value.astype(BF)
            )

    twin_node = remote(node_mine, node_other, twin_send.at[1], twin_recv.at[1], twin)
    twin_node.start()
    reducer_e.to_gather()
    reducer_e.forward()
    twin_new.wait()
    twin_node.wait()
    for j in range(4):

        @pl.when(inside(here - DISTANCES[j], dom_count))
        def _():
            home_copy(j, here - DISTANCES[j]).wait_send()

    reducer_e.finish()


def unpack_kernel(final_n, final_e, node_mine, node_other, new_mine, new_other, *outs):
    new_nodes, node_grads, dew1, deb, dew2, dnw1, dnb, dnw2, dgain = outs
    core = lax.axis_index("sub")
    half = new_mine.shape[0]
    new_nodes[pl.ds(pl.multiple_of(core * half, BLOCK), half), :] = new_mine[...]
    new_nodes[pl.ds(pl.multiple_of((1 - core) * half, BLOCK), half), :] = new_other[...]
    node_grads[...] = (node_mine[...].astype(F32) + node_other[...].astype(F32)).astype(BF)
    tall, quarter = dew1.shape
    ends = []
    for final, out in ((final_e, dew1), (final_n, dnw1)):
        at = 0
        for c in range(0, quarter, 128):
            out[:, c : c + 128] = final[at : at + tall, :].astype(F32)
            at += tall
        ends.append(at)
    at = ends[1]
    for out in (dew2, dnw2):
        out[...] = final_n[at : at + quarter, :].astype(F32)
        at += quarter
    tail_n = final_n[at : at + 16, :].astype(F32)
    tail_e = final_e[ends[0] : ends[0] + 16, :].astype(F32)
    n = quarter // 128
    for c in range(n):
        deb[:, c * 128 : (c + 1) * 128] = tail_e[c : c + 1, :]
        dnb[:, c * 128 : (c + 1) * 128] = tail_n[c : c + 1, :]
    dgain[...] = tail_n[n : n + 1, :]


def on_device(
    dom_count,
    case_count,
    node_feats,
    cotangent,
    block_counts,
    neighbours,
    send_sets,
    edge_w1,
    edge_b1,
    edge_w2,
    node_w1,
    node_b1,
    node_w2,
    norm_gain,
):
    _, rows, width = node_feats.shape
    block_count, fan = neighbours.shape
    bound = send_sets.shape[1]
    quarter = edge_w1.shape[1]
    wide = 2 * quarter
    ext_count = block_count + 4 * bound
    half = rows // 2
    edges = block_count // 2 * fan
    vmem = pl.BlockSpec(memory_space=pltpu.VMEM)
    smem = pl.BlockSpec(memory_space=pltpu.SMEM)
    anywhere = pl.BlockSpec(memory_space=pl.ANY)
    shape = jax.ShapeDtypeStruct
    dma = pltpu.SemaphoreType.DMA
    feats = node_feats.reshape(block_count, BLOCK, width)
    cot = cotangent.reshape(block_count, BLOCK, width)
    eb = edge_b1.reshape(1, quarter)
    nb = node_b1.reshape(1, quarter)
    gain = norm_gain.reshape(1, width)

    prev, last = pl.pallas_call(
        chain_kernel,
        out_shape=[shape((edges,), jnp.int32), shape((ext_count,), jnp.int32)],
        in_specs=[smem],
        out_specs=[smem, smem],
        name="chain",
    )(neighbours)

    def padded(count):
        unit = 16 * dom_count * case_count
        return -(-(count + 16) // unit) * unit

    def reducer_scratch(total):
        slab = total // case_count
        piece = slab // dom_count
        count = case_count + 2 * (dom_count - 1) + (case_count - 1) * dom_count
        return [
            pltpu.VMEM((total, 128), F32),
            pltpu.VMEM((total, 128), BF),
            pltpu.VMEM((total, 128), BF),
            pltpu.VMEM((case_count - 1, slab, 128), BF),
            pltpu.VMEM((case_count - 1, slab, 128), BF),
            pltpu.VMEM((slab, 128), BF),
            pltpu.VMEM((dom_count - 1, piece, 128), BF),
            dma((count,)),
            dma((count,)),
        ]

    total_n = padded(4 * quarter)
    total_e = padded(2 * quarter)
    blocks = (4, bound, BLOCK, width)
    results = pl.pallas_call(
        functools.partial(layer_kernel, dom_count, case_count, bound),
        out_shape=[
            shape((total_n, 128), BF),
            shape((total_e, 128), BF),
            shape((rows, width), BF),
            shape((rows, width), BF),
            shape((half, width), BF),
            shape((half, width), BF),
        ],
        in_specs=[smem] * 5 + [anywhere] * 9,
        out_specs=[vmem] * 6,
        scratch_shapes=reducer_scratch(total_n)
        + reducer_scratch(total_e)
        + [
            pltpu.VMEM((block_count, BLOCK, width), BF),
            pltpu.VMEM((block_count, BLOCK, width), BF),
            pltpu.VMEM((1, width), F32),
            pltpu.VMEM(blocks, BF),
            pltpu.VMEM(blocks, BF),
            pltpu.VMEM((ext_count, BLOCK, width), BF),
            pltpu.VMEM((2 * width, wide), BF),
            pltpu.VMEM((1, wide), F32),
            pltpu.VMEM((wide, width), BF),
            pltpu.VMEM((2 * width, wide), BF),
            pltpu.VMEM((1, wide), F32),
            pltpu.VMEM((wide, width), BF),
            pltpu.VMEM((2 * width, wide), BF),
            pltpu.VMEM((ext_count, BLOCK, wide), F32),
            pltpu.VMEM((BLOCK, wide), F32),
            pltpu.VMEM((edges * BLOCK, wide), BF),
            pltpu.VMEM((half, wide), F32),
            pltpu.VMEM((half, wide), BF),
            pltpu.VMEM((half, 2 * width), BF),
            pltpu.VMEM((half, wide), BF),
            pltpu.VMEM((half, width), BF),
            pltpu.VMEM((half, wide), BF),
            pltpu.VMEM((half, width), BF),
            pltpu.VMEM((half, wide), BF),
            pltpu.VMEM((half, width), F32),
            pltpu.VMEM((width, wide), F32),
            pltpu.VMEM((1, width), F32),
            pltpu.VMEM((fan * BLOCK, width), BF),
            pltpu.VMEM((edges + 1, BLOCK, width), F32),
            pltpu.VMEM(blocks, BF),
            pltpu.VMEM(blocks, BF),
            dma((9,)),
            dma((6,)),
            dma((6,)),
            dma((4,)),
            dma((4,)),
            dma((4,)),
            dma((4,)),
            dma((2,)),
            dma((2,)),
        ],
        compiler_params=pltpu.CompilerParams(
            collective_id=0, has_side_effects=True, vmem_limit_bytes=48 << 20
        ),
        name="layer",
    )(
        send_sets, block_counts, neighbours, prev, last, feats, cot, gain,
        edge_w1, eb, edge_w2, node_w1, nb, node_w2,
    )

    outs = pl.pallas_call(
        unpack_kernel,
        out_shape=[
            shape((rows, width), BF),
            shape((rows, width), BF),
            shape((2 * width, quarter), F32),
            shape((1, quarter), F32),
            shape((quarter, width), F32),
            shape((2 * width, quarter), F32),
            shape((1, quarter), F32),
            shape((quarter, width), F32),
            shape((1, width), F32),
        ],
        in_specs=[vmem] * 6,
        out_specs=[vmem] * 9,
        compiler_params=pltpu.CompilerParams(vmem_limit_bytes=16 << 20),
        name="unpack",
    )(*results)
    return (
        outs[0][None],
        outs[1][None],
        outs[2],
        outs[3].reshape(quarter),
        outs[4],
        outs[5],
        outs[6].reshape(quarter),
        outs[7],
        outs[8].reshape(width),
    )


def solution(mesh):
    placed = (
        P(("groups", "case"), "dom", None),
        P(("groups", "case"), "dom", None),
        P(("groups", "dom")),
        P(("groups", "dom"), None),
        P(("groups", "dom"), None),
        P(None, "sub"),
        P("sub"),
        P("sub", None),
        P(None, "sub"),
        P("sub"),
        P("sub", None),
        P(),
    )
    return jax.shard_map(
        functools.partial(on_device, mesh.shape["dom"], mesh.shape["case"]),
        mesh=mesh,
        in_specs=placed,
        out_specs=(
            P(("groups", "case"), "dom", None),
            P(("groups", "case"), "dom", None),
            P("groups", "sub"),
            P(("groups", "sub")),
            P(("groups", "sub"), None),
            P("groups", "sub"),
            P(("groups", "sub")),
            P(("groups", "sub"), None),
            P("groups"),
        ),
        check_vma=False,
    )
```

time: 69.7 us -> 70.7 us (1.014)
  Pallas kernels: 60.3 us -> 61.3 us
    pallas_call x3 -> x2, Pallas kernels: 59.2 us -> 60.2 us  [the longest x1 57.8 us: on_device(): pl.pallas_call(functools.partial(layer_kernel, dom_count, case_count, bou...]
    unnamed x34 -> x30, local copies, waits for them, and re-layouts: 7.52 us -> 7.56 us
where the time goes in v2:
time: 70.7 us; the launch traced here: 70.3 us
  Pallas kernels  61.3 us (87%)
  local copies, waits for them, and re-layouts  7.56 us (11%)
  between operations  1.38 us (2%)
    pallas_call x1, Pallas kernels, on_device(): pl.pallas_call(functools.partial(layer_kernel, dom_count, case_count, bou...  57.8 us
    unnamed x30, local copies, waits for them, and re-layouts  7.56 us
    pallas_call x1, Pallas kernels, on_device(): pl.pallas_call(chain_kernel, out_shape=[shape((edges,), jnp.int32), shape...  2.34 us

profile of v2, /device:TPU:0, one launch (start us, length us, event | category | flops | bytes accessed | tf_op | source)
XLA Modules:
  0.0 70.3 jit_solution(691347564082351622)
XLA Ops:
  1.3 0.0 copy-start.12
  1.3 0.0 copy-start.13
  1.3 0.7 copy-done.13
  2.0 0.1 copy.22.refs_0_
  2.1 0.0 copy-done.12
  2.1 0.7 copy.23.links.refs_2_
  2.8 2.3 %chain.1 = (s32[40]{0:T(128)}, s32[18]{0:T(128)}) custom-call(s32[10,8]{1,0:T(8,128)} %copy.23.links.refs_2_), custom_call_target="tpu_custom_call" | custom-call | tf_op jit(solution)/shard_map/chain/pallas_call | solution.py:553
  5.1 0.0 copy-start.8
  5.1 0.0 copy-start.10
  5.1 0.0 copy-start.11
  5.1 0.0 copy-start.7
  5.2 0.0 copy-start.9
  5.2 0.6 copy-done.8
  5.8 0.0 copy-done.11
  5.8 0.0 copy-done.7
  5.8 0.0 copy-done.9
  5.8 1.0 %copy-done = bf16[1,1280,128]{2,1,0:T(8,128)(2,1)S(1)} copy-done((bf16[1,1280,128]{2,1,0:T(8,128)(2,1)S(1)}, bf16[1,1280,128]{2,1,0:T(8,128)(2,1)}, u32[]{:S(2)}) %copy-start) | copy-done | bytes 327704
  6.8 1.0 %copy-done.1 = bf16[1,1280,128]{2,1,0:T(8,128)(2,1)S(1)} copy-done((bf16[1,1280,128]{2,1,0:T(8,128)(2,1)S(1)}, bf16[1,1280,128]{2,1,0:T(8,128)(2,1)}, u32[]{:S(2)}) %copy-start.1) | copy-done | bytes 327704
  7.8 0.9 %copy-done.2 = bf16[256,256]{1,0:T(8,128)(2,1)S(1)} copy-done((bf16[256,256]{1,0:T(8,128)(2,1)S(1)}, bf16[256,256]{1,0:T(8,128)(2,1)}, u32[]{:S(2)}) %copy-start.2) | copy-done | bytes 131096
  8.7 0.9 %copy-done.3 = bf16[256,256]{1,0:T(8,128)(2,1)S(1)} copy-done((bf16[256,256]{1,0:T(8,128)(2,1)S(1)}, bf16[256,256]{1,0:T(8,128)(2,1)}, u32[]{:S(2)}) %copy-start.3) | copy-done | bytes 131096
  9.6 0.8 %copy-done.5 = bf16[256,128]{1,0:T(8,128)(2,1)S(1)} copy-done((bf16[256,128]{1,0:T(8,128)(2,1)S(1)}, bf16[256,128]{1,0:T(8,128)(2,1)}, u32[]{:S(2)}) %copy-start.5) | copy-done | bytes 65560
  10.4 0.8 %copy-done.6 = bf16[256,128]{1,0:T(8,128)(2,1)S(1)} copy-done((bf16[256,128]{1,0:T(8,128)(2,1)S(1)}, bf16[256,128]{1,0:T(8,128)(2,1)}, u32[]{:S(2)}) %copy-start.6) | copy-done | bytes 65560
  11.3 57.8 %layer.1 = (bf16[1152,128]{1,0:T(8,128)(2,1)S(1)}, bf16[640,128]{1,0:T(8,128)(2,1)S(1)}, bf16[1280,128]{1,0:T(8,128)(2,1)S(1)}, bf16[1280,128]{1,0:T(8,128)(2,1)...) custom-call(s32[4,2]{1,0:T(4,128)S(1)} %copy.22.refs_0_, s32[1]{0:T(128)S(6)} %copy.24.refs_1_, ...), custom_call_target="tpu_custom_call" | custom-call | tf_op jit(solution)/shard_map/layer/pallas_call | solution.py:584
  69.1 1.2 %unpack.1 = (bf16[1280,128]{1,0:T(8,128)(2,1)}, bf16[1280,128]{1,0:T(8,128)(2,1)}, f32[256,256]{1,0:T(8,128)}, f32[1,256]{1,0:T(1,128)}, f32[256,128]{1,0:T(8,12...) custom-call(bf16[1152,128]{1,0:T(8,128)(2,1)S(1)} %get-tuple-element.28.final_n, ...), custom_call_target="tpu_custom_call" | custom-call | tf_op jit(solution)/shard_map/unpack/pallas_call | solution.py:649
  (9 shorter events, 0.0 us)
Async XLA Ops:
  1.3 0.8 %copy-start.12 = (s32[10,8]{0,1:T(8,128)S(1)}, s32[10,8]{0,1:T(8,128)}, u32[]{:S(2)}) copy-start(s32[10,8]{0,1:T(8,128)} %param.15) | copy-start | bytes 964
  1.3 0.7 copy-start.13
  2.8 2.4 %copy-start.4 = (s32[10,8]{1,0:T(8,128)S(1)}, s32[10,8]{1,0:T(8,128)}, u32[]{:S(2)}) copy-start(s32[10,8]{1,0:T(8,128)} %copy.23.links.refs_2_) | copy-start | bytes 964
  5.1 0.7 copy-start.8
  5.1 0.7 copy-start.10
  5.1 0.7 copy-start.11
  5.1 0.7 copy-start.7
  5.2 0.7 copy-start.9
  5.8 1.0 %copy-start = (bf16[1,1280,128]{2,1,0:T(8,128)(2,1)S(1)}, bf16[1,1280,128]{2,1,0:T(8,128)(2,1)}, u32[]{:S(2)}) copy-start(bf16[1,1280,128]{2,1,0:T(8,128)(2,1)} %param.12) | copy-start | bytes 983044
  6.8 1.0 %copy-start.1 = (bf16[1,1280,128]{2,1,0:T(8,128)(2,1)S(1)}, bf16[1,1280,128]{2,1,0:T(8,128)(2,1)}, u32[]{:S(2)}) copy-start(bf16[1,1280,128]{2,1,0:T(8,128)(2,1)} %param.13) | copy-start | bytes 983044
  7.8 0.9 %copy-start.2 = (bf16[256,256]{1,0:T(8,128)(2,1)S(1)}, bf16[256,256]{1,0:T(8,128)(2,1)}, u32[]{:S(2)}) copy-start(bf16[256,256]{1,0:T(8,128)(2,1)} %refs_8_.1) | copy-start | bytes 393220
  8.7 0.9 %copy-start.3 = (bf16[256,256]{1,0:T(8,128)(2,1)S(1)}, bf16[256,256]{1,0:T(8,128)(2,1)}, u32[]{:S(2)}) copy-start(bf16[256,256]{1,0:T(8,128)(2,1)} %refs_11_.1) | copy-start | bytes 393220
  9.6 0.8 %copy-start.5 = (bf16[256,128]{1,0:T(8,128)(2,1)S(1)}, bf16[256,128]{1,0:T(8,128)(2,1)}, u32[]{:S(2)}) copy-start(bf16[256,128]{1,0:T(8,128)(2,1)} %refs_10_.1) | copy-start | bytes 196612
  10.4 0.8 %copy-start.6 = (bf16[256,128]{1,0:T(8,128)(2,1)S(1)}, bf16[256,128]{1,0:T(8,128)(2,1)}, u32[]{:S(2)}) copy-start(bf16[256,128]{1,0:T(8,128)(2,1)} %refs_13_.1) | copy-start | bytes 196612

commit v3 on v2

--- a/solution.py
+++ b/solution.py
@@ -49,15 +49,15 @@
     own = block_count // 2
     none = own * fan
 
-    @pl.loop(0, last_o.shape[0])
-    def _(s):
+    for s in range(last_o.shape[0]):
         last_o[s] = none
 
-    @pl.loop(0, none)
-    def _(e):
-        source = jnp.maximum(links[core * own + e // fan, lax.rem(e, fan)], 0)
-        prev_o[e] = last_o[source]
-        last_o[source] = e
+    @pl.loop(0, own)
+    def _(i):
+        for k in range(fan):
+            source = jnp.maximum(links[core * own + i, k], 0)
+            prev_o[i * fan + k] = last_o[source]
+            last_o[source] = i * fan + k
 
 
 class Reducer:
@@ -174,6 +174,13 @@
     for piece in pieces:
         out[at : at + piece.shape[0], :] = piece.astype(out.dtype)
         at += piece.shape[0]
+    if lines:
+        fill_lines(out, at, lines)
+    elif at < out.shape[0]:
+        out[at:, :] = jnp.zeros((out.shape[0] - at, 128), out.dtype)
+
+
+def fill_lines(out, at, lines):
     lines = lines + [jnp.zeros((16 - len(lines), 128), F32)]
     out[at : at + 16, :] = jnp.concatenate(lines, axis=0).astype(out.dtype)
     at += 16
@@ -376,7 +383,7 @@
         fill(
             out,
             columns(dnode, lo, hi) + [dew2[lo:hi, :], dnw2[lo:hi, :]],
-            columns(dnb, lo, hi) + [dgain_row],
+            [],
         )
     reducer_n.to_sub()
 
@@ -406,11 +413,10 @@
             chain[e] = spread[k * BLOCK : (k + 1) * BLOCK, :] + chain[prev[e]]
         dsrc[...] += dot_tn(srcs[...], g)
 
-    steps = [reducer_n.to_case, reducer_n.to_dom, reducer_n.to_gather, reducer_n.forward]
-    for n, step in enumerate(steps):
-        pl.loop(min(n, own), min(n + 1, own))(backward)
-        step()
-    pl.loop(min(len(steps), own), own)(backward)
+    first = min(2, own)
+    pl.loop(0, first)(backward)
+    reducer_n.to_case()
+    pl.loop(first, own)(backward)
 
     def home_copy(j, there):
         return remote(
@@ -430,13 +436,13 @@
     for out, lo in ((reducer_e.other, quarter), (reducer_e.mine, 0)):
         hi = lo + quarter
         both = zip(columns(dtgt, lo, hi), columns(dsrc[...], lo, hi))
-        fill(out, [x for pieces in both for x in pieces], columns(deb, lo, hi))
+        lines = columns(deb, lo, hi) + columns(dnb, lo, hi) + [dgain_row]
+        fill(out, [x for pieces in both for x in pieces], lines)
         if lo > 0:
             reducer_e.to_sub()
-    reducer_e.to_case()
-    reducer_n.finish()
-
+    reducer_n.to_dom()
     part = psrc
+
     @pl.loop(0, block_count)
     def _(b):
         part[b, :, :width] = chain[last[b]]
@@ -446,13 +452,14 @@
         rows = block_rows(i)
         part[core * own + i, :, :width] += gxnode[rows, :] + dot_nt(tgrad[rows, :], w1f[:width, :])
 
+    reducer_e.to_case()
+    reducer_n.to_gather()
     for j in range(4):
 
         @pl.when(inside(here + DISTANCES[j], dom_count))
         def _():
             home_copy(j, here + DISTANCES[j]).wait_recv()
 
-    reducer_e.to_dom()
     hits = [
         [jnp.where(send[j, m] == b, 1.0, 0.0) for j in range(4) for m in range(bound)]
         for b in range(block_count)
@@ -474,8 +481,11 @@
 
     twin_node = remote(node_mine, node_other, twin_send.at[1], twin_recv.at[1], twin)
     twin_node.start()
+    reducer_e.to_dom()
+    reducer_n.forward()
     reducer_e.to_gather()
     reducer_e.forward()
+    reducer_n.finish()
     twin_new.wait()
     twin_node.wait()
     for j in range(4):
@@ -503,16 +513,15 @@
             at += tall
         ends.append(at)
     at = ends[1]
+    tail = final_e[ends[0] : ends[0] + 16, :].astype(F32)
     for out in (dew2, dnw2):
         out[...] = final_n[at : at + quarter, :].astype(F32)
         at += quarter
-    tail_n = final_n[at : at + 16, :].astype(F32)
-    tail_e = final_e[ends[0] : ends[0] + 16, :].astype(F32)
     n = quarter // 128
     for c in range(n):
-        deb[:, c * 128 : (c + 1) * 128] = tail_e[c : c + 1, :]
-        dnb[:, c * 128 : (c + 1) * 128] = tail_n[c : c + 1, :]
-    dgain[...] = tail_n[n : n + 1, :]
+        deb[:, c * 128 : (c + 1) * 128] = tail[c : c + 1, :]
+        dnb[:, c * 128 : (c + 1) * 128] = tail[n + c : n + c + 1, :]
+    dgain[...] = tail[2 * n : 2 * n + 1, :]
 
 
 def on_device(
@@ -560,7 +569,7 @@
 
     def padded(count):
         unit = 16 * dom_count * case_count
-        return -(-(count + 16) // unit) * unit
+        return -(-count // unit) * unit
 
     def reducer_scratch(total):
         slab = total // case_count
@@ -578,8 +587,8 @@
             dma((count,)),
         ]
 
-    total_n = padded(4 * quarter)
-    total_e = padded(2 * quarter)
+    total_n = padded(2 * width * quarter // 128 + 2 * quarter)
+    total_e = padded(2 * width * quarter // 128 + 16)
     blocks = (4, bound, BLOCK, width)
     results = pl.pallas_call(
         functools.partial(layer_kernel, dom_count, case_count, bound),

time: 70.7 us -> 64.2 us (0.908)
  Pallas kernels: 61.3 us -> 54.8 us
    pallas_call x1, Pallas kernels: 57.8 us -> 52.1 us  [on_device(): pl.pallas_call(functools.partial(layer_kernel, dom_count, case_count, bou...]
    pallas_call x1, Pallas kernels: 2.34 us -> 1.59 us  [on_device(): pl.pallas_call(chain_kernel, out_shape=[shape((edges,), jnp.int32), shape...]
where the time goes in v3:
time: 64.2 us; the launch traced here: 63.7 us
  Pallas kernels  54.8 us (85%)
  local copies, waits for them, and re-layouts  7.56 us (12%)
  between operations  1.38 us (2%)
    pallas_call x1, Pallas kernels, on_device(): pl.pallas_call(functools.partial(layer_kernel, dom_count, case_count, bou...  52.1 us
    unnamed x30, local copies, waits for them, and re-layouts  7.56 us
    pallas_call x1, Pallas kernels, on_device(): pl.pallas_call(chain_kernel, out_shape=[shape((edges,), jnp.int32), shape...  1.59 us

profile of v3, /device:TPU:0, one launch (start us, length us, event | category | flops | bytes accessed | tf_op | source)
XLA Modules:
  0.0 63.7 jit_solution(747468540400454508)
XLA Ops:
  1.3 0.0 copy-start.12
  1.3 0.0 copy-start.13
  1.3 0.7 %copy-done.13 = s32[4,2]{0,1:T(2,128)S(1)} copy-done((s32[4,2]{0,1:T(2,128)S(1)}, s32[4,2]{0,1:T(2,128)}, u32[]{:S(2)}) %copy-start.13) | copy-done | bytes 56
  2.0 0.1 copy.22.refs_0_
  2.1 0.0 copy-done.12
  2.1 0.7 %copy.23.links.refs_2_ = s32[10,8]{1,0:T(8,128)} copy(s32[10,8]{0,1:T(8,128)S(1)} %copy-done.12) | data formatting | bytes 640 | tf_op args[3]
  2.8 1.6 %chain.1 = (s32[40]{0:T(128)}, s32[18]{0:T(128)}) custom-call(s32[10,8]{1,0:T(8,128)} %copy.23.links.refs_2_), custom_call_target="tpu_custom_call" | custom-call | tf_op jit(solution)/shard_map/chain/pallas_call | solution.py:562
  4.4 0.0 copy-start.8
  4.4 0.0 copy-start.10
  4.4 0.0 copy-start.11
  4.4 0.0 copy-start.7
  4.4 0.0 copy-start.9
  4.4 0.0 copy-done.4
  4.4 0.6 copy-done.8
  5.0 0.0 copy-done.11
  5.0 0.0 copy-done.7
  5.1 1.0 %copy-done = bf16[1,1280,128]{2,1,0:T(8,128)(2,1)S(1)} copy-done((bf16[1,1280,128]{2,1,0:T(8,128)(2,1)S(1)}, bf16[1,1280,128]{2,1,0:T(8,128)(2,1)}, u32[]{:S(2)}) %copy-start) | copy-done | bytes 327704
  6.1 1.0 %copy-done.1 = bf16[1,1280,128]{2,1,0:T(8,128)(2,1)S(1)} copy-done((bf16[1,1280,128]{2,1,0:T(8,128)(2,1)S(1)}, bf16[1,1280,128]{2,1,0:T(8,128)(2,1)}, u32[]{:S(2)}) %copy-start.1) | copy-done | bytes 327704
  7.0 0.9 %copy-done.2 = bf16[256,256]{1,0:T(8,128)(2,1)S(1)} copy-done((bf16[256,256]{1,0:T(8,128)(2,1)S(1)}, bf16[256,256]{1,0:T(8,128)(2,1)}, u32[]{:S(2)}) %copy-start.2) | copy-done | bytes 131096
  7.9 0.9 %copy-done.3 = bf16[256,256]{1,0:T(8,128)(2,1)S(1)} copy-done((bf16[256,256]{1,0:T(8,128)(2,1)S(1)}, bf16[256,256]{1,0:T(8,128)(2,1)}, u32[]{:S(2)}) %copy-start.3) | copy-done | bytes 131096
  8.8 0.8 %copy-done.5 = bf16[256,128]{1,0:T(8,128)(2,1)S(1)} copy-done((bf16[256,128]{1,0:T(8,128)(2,1)S(1)}, bf16[256,128]{1,0:T(8,128)(2,1)}, u32[]{:S(2)}) %copy-start.5) | copy-done | bytes 65560
  9.7 0.8 %copy-done.6 = bf16[256,128]{1,0:T(8,128)(2,1)S(1)} copy-done((bf16[256,128]{1,0:T(8,128)(2,1)S(1)}, bf16[256,128]{1,0:T(8,128)(2,1)}, u32[]{:S(2)}) %copy-start.6) | copy-done | bytes 65560
  10.5 52.1 %layer.1 = (bf16[1024,128]{1,0:T(8,128)(2,1)S(1)}, bf16[640,128]{1,0:T(8,128)(2,1)S(1)}, bf16[1280,128]{1,0:T(8,128)(2,1)S(1)}, bf16[1280,128]{1,0:T(8,128)(2,1)...) custom-call(s32[4,2]{1,0:T(4,128)S(1)} %copy.22.refs_0_, s32[1]{0:T(128)S(6)} %copy.24.refs_1_, ...), custom_call_target="tpu_custom_call" | custom-call | tf_op jit(solution)/shard_map/layer/pallas_call | solution.py:593
  62.6 1.2 %unpack.1 = (bf16[1280,128]{1,0:T(8,128)(2,1)}, bf16[1280,128]{1,0:T(8,128)(2,1)}, f32[256,256]{1,0:T(8,128)}, f32[1,256]{1,0:T(1,128)}, f32[256,128]{1,0:T(8,12...) custom-call(bf16[1024,128]{1,0:T(8,128)(2,1)S(1)} %get-tuple-element.28.final_n, ...), custom_call_target="tpu_custom_call" | custom-call | tf_op jit(solution)/shard_map/unpack/pallas_call | solution.py:658
  (9 shorter events, 0.0 us)
Async XLA Ops:
  1.3 0.8 %copy-start.12 = (s32[10,8]{0,1:T(8,128)S(1)}, s32[10,8]{0,1:T(8,128)}, u32[]{:S(2)}) copy-start(s32[10,8]{0,1:T(8,128)} %param.15) | copy-start | bytes 964
  1.3 0.7 %copy-start.13 = (s32[4,2]{0,1:T(2,128)S(1)}, s32[4,2]{0,1:T(2,128)}, u32[]{:S(2)}) copy-start(s32[4,2]{0,1:T(2,128)} %param.16) | copy-start | bytes 100
  2.8 1.7 %copy-start.4 = (s32[10,8]{1,0:T(8,128)S(1)}, s32[10,8]{1,0:T(8,128)}, u32[]{:S(2)}) copy-start(s32[10,8]{1,0:T(8,128)} %copy.23.links.refs_2_) | copy-start | bytes 964
  4.4 0.7 %copy-start.8 = (f32[256]{0:T(256)S(1)}, f32[256]{0:T(256)}, u32[]{:S(2)}) copy-start(f32[256]{0:T(256)} %param.21) | copy-start | bytes 3076
  4.4 0.7 %copy-start.10 = (s32[40]{0:T(128)S(1)}, s32[40]{0:T(128)}, u32[]{:S(2)}) copy-start(s32[40]{0:T(128)} %get-tuple-element.26.refs_3_) | copy-start | bytes 484
  4.4 0.7 %copy-start.11 = (s32[18]{0:T(128)S(1)}, s32[18]{0:T(128)}, u32[]{:S(2)}) copy-start(s32[18]{0:T(128)} %get-tuple-element.27.refs_4_) | copy-start | bytes 220
  4.4 0.7 %copy-start.7 = (f32[256]{0:T(256)S(1)}, f32[256]{0:T(256)}, u32[]{:S(2)}) copy-start(f32[256]{0:T(256)} %param.18) | copy-start | bytes 3076
  4.4 0.7 %copy-start.9 = (f32[128]{0:T(128)S(1)}, f32[128]{0:T(128)}, u32[]{:S(2)}) copy-start(f32[128]{0:T(128)} %param.23) | copy-start | bytes 1540
  5.1 1.0 %copy-start = (bf16[1,1280,128]{2,1,0:T(8,128)(2,1)S(1)}, bf16[1,1280,128]{2,1,0:T(8,128)(2,1)}, u32[]{:S(2)}) copy-start(bf16[1,1280,128]{2,1,0:T(8,128)(2,1)} %param.12) | copy-start | bytes 983044
  6.1 1.0 %copy-start.1 = (bf16[1,1280,128]{2,1,0:T(8,128)(2,1)S(1)}, bf16[1,1280,128]{2,1,0:T(8,128)(2,1)}, u32[]{:S(2)}) copy-start(bf16[1,1280,128]{2,1,0:T(8,128)(2,1)} %param.13) | copy-start | bytes 983044
  7.0 0.9 %copy-start.2 = (bf16[256,256]{1,0:T(8,128)(2,1)S(1)}, bf16[256,256]{1,0:T(8,128)(2,1)}, u32[]{:S(2)}) copy-start(bf16[256,256]{1,0:T(8,128)(2,1)} %refs_8_.1) | copy-start | bytes 393220
  7.9 0.9 %copy-start.3 = (bf16[256,256]{1,0:T(8,128)(2,1)S(1)}, bf16[256,256]{1,0:T(8,128)(2,1)}, u32[]{:S(2)}) copy-start(bf16[256,256]{1,0:T(8,128)(2,1)} %refs_11_.1) | copy-start | bytes 393220
  8.8 0.8 %copy-start.5 = (bf16[256,128]{1,0:T(8,128)(2,1)S(1)}, bf16[256,128]{1,0:T(8,128)(2,1)}, u32[]{:S(2)}) copy-start(bf16[256,128]{1,0:T(8,128)(2,1)} %refs_10_.1) | copy-start | bytes 196612
  9.7 0.8 %copy-start.6 = (bf16[256,128]{1,0:T(8,128)(2,1)S(1)}, bf16[256,128]{1,0:T(8,128)(2,1)}, u32[]{:S(2)}) copy-start(bf16[256,128]{1,0:T(8,128)(2,1)} %refs_13_.1) | copy-start | bytes 196612
